TPU v7x, 128 devices: a whole 4x4x4 slice. The times are simulated.
128 devices in a mesh: row: 8 (over y, core), col: 16 (over x, z).
Axes of the slice: x: 4, y: 4, z: 4, core: 2. Of those that a mesh axis runs over, the one named last changes fastest.
Arguments:
- embeddings: float32 [131072, 1024], P(('row', 'col')), may hold values from -6 to 6
- neighbour_ids: int32 [256, 12], P(('row', 'col')), may hold values from 0 to 255, as said below
- start_vectors: float32 [131072, 64], P(('row', 'col')), may hold values from -15 to 15
Outputs:
- spectral_vectors: float32 [131072, 64], P(('row', 'col'))
Inputs may be any that keep to these rules, and one draw needn't show every extreme that they name: `neighbour_ids`: slot 0 of block b is b itself. The other slots of block b name distinct blocks other than b held by devices of the same row index whose col index differs from that of b's device by at most 2 cyclically, followed by padding slots that repeat b. Block b sits on device b // 2, with device index row * 16 + col.
All inputs are finite; a program needn't handle non-finite values.
Results may differ from a plain program's by a relative error of at most 0.005.
Values may be sent and summed in bfloat16 or wider, within the bound.
A program may use at most 128 MiB of HBM per device.

v0:
```python
import math

import jax
import jax.numpy as jnp
from jax import lax
from jax.sharding import Mesh
from jax.sharding import PartitionSpec as P

D = 1024
BS = 512
SLOTS = 12
REACH = 2
ITERS = 3
BLK_DEV = 2
COL = ("col_0", "col_1")
ROW_COL = ("row_0", "row_1", "col_0", "col_1")
ROW = ("row_0", "row_1")


SHARP = 8.0
EPSILON = 1e-06


def passed_along(shard, axis, by):
    count = lax.axis_size(axis)
    return lax.ppermute(shard, axis, [(i, (i + by) % count) for i in range(count)])


def sent_to_all(shard, axis):
    count = lax.axis_size(axis)
    return lax.all_to_all(
        jnp.broadcast_to(shard[None], (count, *shard.shape)), axis, 0, 0, tiled=True
    )


def over_copies(shard, axis):
    return sent_to_all(shard, axis).sum(axis=0)


def by_axis(shard, axes):
    far, near = axes
    nearer = over_copies(shard, near)
    return over_copies(nearer, far)


def unit_rows(points):
    rms_inverse = lax.rsqrt(jnp.mean(points * points, axis=-1, keepdims=True) + EPSILON)
    return (points * rms_inverse).astype(jnp.bfloat16)


def band_index(neighbour_ids, col_count, col_index):
    holder = neighbour_ids // BLK_DEV
    offset = (holder % col_count - col_index + col_count + REACH) % col_count
    return offset * BLK_DEV + neighbour_ids % BLK_DEV


def assemble(pieces):
    return jnp.concatenate([pieces[offset] for offset in range(-REACH, REACH + 1)], axis=0)


def point_band(normed):
    pieces = {0: normed}
    for offset in [shifted for shifted in range(-REACH, REACH + 1) if shifted != 0]:
        pieces[offset] = passed_along(normed, COL, -offset)
    return assemble(pieces)


def vector_band(scaled):
    pieces = {0: scaled}
    for offset in [shifted for shifted in range(-REACH, REACH + 1) if shifted != 0]:
        pieces[offset] = passed_along(scaled, COL, -offset)
    return assemble(pieces)


def orthonormal(image_rows, total_rows):
    gram_sum = lax.dot_general(
        image_rows,
        image_rows,
        (((0,), (0,)), ((), ())),
        precision=lax.Precision.HIGHEST,
        preferred_element_type=jnp.float32,
    )
    gram_sum = by_axis(gram_sum, (("row_0", "row_1"), ("col_0", "col_1")))
    factor = jnp.linalg.cholesky(gram_sum)
    solved = lax.linalg.triangular_solve(
        factor, image_rows, left_side=False, lower=True, transpose_a=True
    )
    return solved * math.sqrt(total_rows)


def on_device(embeddings, neighbour_ids, start_vectors):
    col_count = lax.axis_size(COL)
    col_index = lax.axis_index(COL)
    device = lax.axis_index(ROW) * col_count + col_index
    total_rows = embeddings.shape[0] * lax.axis_size(ROW) * col_count
    normed = unit_rows(embeddings)
    point_rows = point_band(normed)
    own_ids = device * BLK_DEV + jnp.arange(BLK_DEV, dtype=jnp.int32)
    slot_ids = jnp.arange(SLOTS, dtype=jnp.int32)
    live_mask = ((slot_ids[None, :] == 0) | (neighbour_ids != own_ids[:, None])).astype(jnp.float32)
    position = band_index(neighbour_ids, col_count, col_index)
    candidates = (2 * REACH + 1) * BLK_DEV
    own_blocks = normed.reshape(BLK_DEV, BS, D)
    tile_list = []
    degree_list = []
    chosen = jnp.sum(
        (position[:, :, None] == jnp.arange(candidates, dtype=jnp.int32)[None, None, :]).astype(
            jnp.float32
        )
        * live_mask[:, :, None],
        axis=1,
    )
    for member in range(BLK_DEV):
        cosine = (
            lax.dot_general(
                own_blocks[member],
                point_rows,
                (((1,), (1,)), ((), ())),
                preferred_element_type=jnp.float32,
            )
            / D
        )
        affinity = (
            jnp.exp(SHARP * (cosine - 1.0)).reshape(BS, candidates, BS)
            * chosen[member][None, :, None]
        )
        degree_list.append(jnp.sum(affinity, axis=(1, 2)))
        tile_list.append(affinity.reshape(BS, candidates * BS).astype(jnp.bfloat16))
    inv_root = lax.rsqrt(jnp.stack(degree_list))
    vectors = start_vectors
    for iteration in range(ITERS):
        scaled = (vectors * inv_root.reshape(-1, 1)).astype(jnp.bfloat16)
        spread = vector_band(scaled)
        image_list = []
        for member in range(BLK_DEV):
            partial_rows = jnp.dot(tile_list[member], spread, preferred_element_type=jnp.float32)
            image_list.append(partial_rows * inv_root[member][:, None])
        image_rows = jnp.concatenate(image_list, axis=0)
        vectors = orthonormal(image_rows, total_rows)
    return vectors


def solution(mesh):
    split = Mesh(mesh.devices.reshape(4, 2, 4, 4), ("row_0", "row_1", "col_0", "col_1"))
    return jax.shard_map(
        on_device,
        mesh=split,
        in_specs=(P(ROW_COL, None), P(ROW_COL, None), P(ROW_COL, None)),
        out_specs=P(ROW_COL, None),
        check_vma=False,
    )
```

profile of v0, /device:TPU:1, one launch (start us, length us, event | category | flops | bytes accessed | tf_op | source)
XLA Modules:
  0.0 394.8 jit_solution(10259792155706293581)
XLA Ops:
  5.1 4.4 %collective-permute-start = (bf16[1024,1024]{1,0:T(8,128)(2,1)}, bf16[1024,1024]{1,0:T(8,128)(2,1)}, u32[]{:S(2)}, u32[]{:S(2)}) collective-permute-start(bf16[1024,1024]{1,0:T(8,128)(2,1)} %multiply_convert_fusion), channel_id=1, source_target_pairs={{0,2},{1,3},{2,4},{3,5},{4,6},{5,7},{6,8},{7,9},{8,10},{9,11},{10,... | collective-permute-start | bytes 6291464 | tf_op jit(solution)/shard_map/ppermute | solution.py:26
  14.9 42.6 %collective-permute-done = bf16[1024,1024]{1,0:T(8,128)(2,1)} collective-permute-done((bf16[1024,1024]{1,0:T(8,128)(2,1)}, bf16[1024,1024]{1,0:T(8,128)(2,1)}, u32[]{:S(2)}, u32[]{:S(2)}) %collective-permute-start) | collective-permute-done | bytes 2097184 | tf_op jit(solution)/shard_map/ppermute | solution.py:26
  60.5 42.0 %collective-permute-done.1 = bf16[1024,1024]{1,0:T(8,128)(2,1)} collective-permute-done((bf16[1024,1024]{1,0:T(8,128)(2,1)}, bf16[1024,1024]{1,0:T(8,128)(2,1)}, u32[]{:S(2)}, u32[]{:S(2)}) %collective-permute-start.1) | collective-permute-done | bytes 2097184 | tf_op jit(solution)/shard_map/ppermute | solution.py:26
  107.2 83.2 %collective-permute-done.2 = bf16[1024,1024]{1,0:T(8,128)(2,1)} collective-permute-done((bf16[1024,1024]{1,0:T(8,128)(2,1)}, bf16[1024,1024]{1,0:T(8,128)(2,1)}, u32[]{:S(2)}, u32[]{:S(2)}) %collective-permute-start.2) | collective-permute-done | bytes 2097184 | tf_op jit(solution)/shard_map/ppermute | solution.py:26
  195.0 10.0 %fusion.45 = (f32[512]{0:T(512)S(1)}, bf16[512,5120]{1,0:T(8,128)(2,1)S(1)}) fusion(f32[5120]{0:T(1024)S(1)} %mul.160, bf16[5120,1024]{1,0:T(8,128)(2,1)} %constant_dynamic-update-slice_fusion, bf16[1024,1024]{1,0:T(8,128)(2,1)} %multiply_convert_fusion), kind=kOutput, calls=%fused_computation.114 | convolution fusion | flops 5384437248 | bytes 16799744 | tf_op jit(solution)/shard_map/dot_general | solution.py:115
  205.0 11.9 %fusion.44 = (f32[512]{0:T(512)S(1)}, bf16[512,5120]{1,0:T(8,128)(2,1)S(1)}) fusion(f32[5120]{0:T(1024)S(1)} %mul.166, bf16[5120,1024]{1,0:T(8,128)(2,1)} %constant_dynamic-update-slice_fusion, bf16[1024,1024]{1,0:T(8,128)(2,1)} %multiply_convert_fusion), kind=kOutput, calls=%fused_computation.113 | convolution fusion | flops 5384437248 | bytes 16799744 | tf_op jit(solution)/shard_map/dot_general | solution.py:115
  217.2 4.8 %collective-permute-start.6 = (bf16[1024,64]{0,1:T(8,128)(2,1)S(1)}, bf16[1024,64]{0,1:T(8,128)(2,1)S(1)}, u32[]{:S(2)}, u32[]{:S(2)}) collective-permute-start(bf16[1024,64]{0,1:T(8,128)(2,1)S(1)} %multiply_convert_fusion.1), channel_id=1, source_target_pairs={{0,15},{1,0},{2,1},{3,2},{4,3},{5,4},{6,5},{7,6},{8,7},{9,8},{10,9... | collective-permute-start | bytes 393224 | tf_op jit(solution)/shard_map/ppermute | solution.py:26
  226.4 4.8 %collective-permute-done.7 = bf16[1024,64]{0,1:T(8,128)(2,1)S(1)} collective-permute-done((bf16[1024,64]{0,1:T(8,128)(2,1)S(1)}, bf16[1024,64]{0,1:T(8,128)(2,1)S(1)}, u32[]{:S(2)}, u32[]{:S(2)}) %collective-permute-start.7) | collective-permute-done | bytes 131104 | tf_op jit(solution)/shard_map/ppermute | solution.py:26
  235.4 10.0 %all_to_all.30 = f32[16,1,4096]{2,1,0:T(1,128)S(1)} all-to-all(f32[16,1,4096]{2,1,0:T(1,128)S(1)} %reshape.74), channel_id=1, replica_groups=mesh['row_0'=4,'row_1'=2,'col_0'=4,'col_1'=4] {'col_0','col_1'}, dimensions={0} | all-to-all | bytes 524288 | tf_op jit(solution)/shard_map/all_to_all | solution.py:31
  248.3 7.9 %all-to-all-start.1 = ((f32[8,1,4096]{2,1,0:T(1,128)}), f32[8,1,4096]{2,1,0:T(1,128)S(1)}, u32[]{:S(2)}, u32[]{:S(2)}) async-start(f32[8,1,4096]{2,1,0:T(1,128)} %reshape.76), calls=%async_computation.1 | async-start | bytes 262144 | tf_op jit(solution)/shard_map/all_to_all | solution.py:31
  256.2 5.3 %all-to-all-done.1 = f32[8,1,4096]{2,1,0:T(1,128)S(1)} async-done(((f32[8,1,4096]{2,1,0:T(1,128)}), f32[8,1,4096]{2,1,0:T(1,128)S(1)}, u32[]{:S(2)}, u32[]{:S(2)}) %all-to-all-start.1) | async-done | bytes 131104 | tf_op jit(solution)/shard_map/all_to_all | solution.py:31
  262.7 5.8 %cholesky.59 = f32[64,64]{1,0:T(8,128)S(1)} custom-call(f32[64,64]{1,0:T(8,128)S(1)} %fusion.18), custom_call_target="Cholesky" | custom-call | tf_op jit(solution)/shard_map/jit(cholesky)/cholesky | solution.py:84
  269.9 4.9 %custom-call.7 = f32[1,64,64]{1,2,0:T(8,128)S(1)} custom-call(f32[1,64,64]{2,1,0:T(8,128)S(1)} %fusion.10), custom_call_target="InvertDiagBlocksLowerTriangular" | custom-call | tf_op jit(solution)/shard_map/triangular_solve/custom-call.0 | solution.py:85
  276.6 4.7 %collective-permute-start.10 = (bf16[1024,64]{0,1:T(8,128)(2,1)S(1)}, bf16[1024,64]{0,1:T(8,128)(2,1)S(1)}, u32[]{:S(2)}, u32[]{:S(2)}) collective-permute-start(bf16[1024,64]{0,1:T(8,128)(2,1)S(1)} %fusion.3), channel_id=1, source_target_pairs={{0,15},{1,0},{2,1},{3,2},{4,3},{5,4},{6,5},{7,6},{8,7},{9,8},{10,9... | collective-permute-start | bytes 393224 | tf_op jit(solution)/shard_map/ppermute | solution.py:26
  295.2 11.2 %all_to_all.31 = f32[16,1,4096]{2,1,0:T(1,128)S(1)} all-to-all(f32[16,1,4096]{2,1,0:T(1,128)S(1)} %reshape.78), channel_id=1, replica_groups=mesh['row_0'=4,'row_1'=2,'col_0'=4,'col_1'=4] {'col_0','col_1'}, dimensions={0} | all-to-all | bytes 524288 | tf_op jit(solution)/shard_map/all_to_all | solution.py:31
  308.1 11.7 %all_to_all.32 = f32[8,1,4096]{2,1,0:T(1,128)S(1)} all-to-all(f32[8,1,4096]{2,1,0:T(1,128)S(1)} %reshape.80), channel_id=1, replica_groups=mesh['row_0'=4,'row_1'=2,'col_0'=4,'col_1'=4] {'row_0','row_1'}, dimensions={0} | all-to-all | bytes 262144 | tf_op jit(solution)/shard_map/all_to_all | solution.py:31
  321.0 5.8 %cholesky.70 = f32[64,64]{1,0:T(8,128)S(1)} custom-call(f32[64,64]{1,0:T(8,128)S(1)} %fusion.16), custom_call_target="Cholesky" | custom-call | tf_op jit(solution)/shard_map/jit(cholesky)/cholesky | solution.py:84
  328.2 4.9 %custom-call.8 = f32[1,64,64]{1,2,0:T(8,128)S(1)} custom-call(f32[1,64,64]{2,1,0:T(8,128)S(1)} %fusion.11), custom_call_target="InvertDiagBlocksLowerTriangular" | custom-call | tf_op jit(solution)/shard_map/triangular_solve/custom-call.0 | solution.py:85
  334.9 4.7 %collective-permute-start.14 = (bf16[1024,64]{0,1:T(8,128)(2,1)S(1)}, bf16[1024,64]{0,1:T(8,128)(2,1)S(1)}, u32[]{:S(2)}, u32[]{:S(2)}) collective-permute-start(bf16[1024,64]{0,1:T(8,128)(2,1)S(1)} %fusion.4), channel_id=1, source_target_pairs={{0,15},{1,0},{2,1},{3,2},{4,3},{5,4},{6,5},{7,6},{8,7},{9,8},{10,9... | collective-permute-start | bytes 393224 | tf_op jit(solution)/shard_map/ppermute | solution.py:26
  351.1 4.2 %convolution_multiply_fusion = f32[512,64]{0,1:T(8,128)S(1)} fusion(bf16[5120,64]{0,1:T(8,128)(2,1)S(1)} %constant_dynamic-update-slice_fusion.15, f32[512]{0:T(512)S(1)} %bitcast.66, bf16[512,5120]{1,0:T(8,128)(2,1)} %copy-done.1), kind=kOutput, calls=%fused_computation.12 | convolution fusion | flops 335577088 | bytes 6031360 | tf_op jit(solution)/shard_map/dot_general | solution.py:136
  356.1 10.9 %all_to_all.33 = f32[16,1,4096]{2,1,0:T(1,128)S(1)} all-to-all(f32[16,1,4096]{2,1,0:T(1,128)S(1)} %reshape.82), channel_id=1, replica_groups=mesh['row_0'=4,'row_1'=2,'col_0'=4,'col_1'=4] {'col_0','col_1'}, dimensions={0} | all-to-all | bytes 524288 | tf_op jit(solution)/shard_map/all_to_all | solution.py:31
  368.7 11.7 %all_to_all.34 = f32[8,1,4096]{2,1,0:T(1,128)S(1)} all-to-all(f32[8,1,4096]{2,1,0:T(1,128)S(1)} %reshape.84), channel_id=1, replica_groups=mesh['row_0'=4,'row_1'=2,'col_0'=4,'col_1'=4] {'row_0','row_1'}, dimensions={0} | all-to-all | bytes 262144 | tf_op jit(solution)/shard_map/all_to_all | solution.py:31
  381.6 5.8 %cholesky.81 = f32[64,64]{1,0:T(8,128)S(1)} custom-call(f32[64,64]{1,0:T(8,128)S(1)} %fusion.14), custom_call_target="Cholesky" | custom-call | tf_op jit(solution)/shard_map/jit(cholesky)/cholesky | solution.py:84
  388.8 4.9 %custom-call.9 = f32[1,64,64]{1,2,0:T(8,128)S(1)} custom-call(f32[1,64,64]{2,1,0:T(8,128)S(1)} %fusion.12), custom_call_target="InvertDiagBlocksLowerTriangular" | custom-call | tf_op jit(solution)/shard_map/triangular_solve/custom-call.0 | solution.py:85
  (133 shorter events, 76.1 us)
Async XLA Ops:
  0.0 3.4 copy-start.3
  0.0 14.3 %copy-start.6 = (s32[2,12]{1,0:T(2,128)S(1)}, s32[2,12]{1,0:T(2,128)}, u32[]{:S(2)}) copy-start(s32[2,12]{1,0:T(2,128)} %param.7) | copy-start | bytes 292
  5.1 52.3 %collective-permute-start = (bf16[1024,1024]{1,0:T(8,128)(2,1)}, bf16[1024,1024]{1,0:T(8,128)(2,1)}, u32[]{:S(2)}, u32[]{:S(2)}) collective-permute-start(bf16[1024,1024]{1,0:T(8,128)(2,1)} %multiply_convert_fusion), channel_id=1, source_target_pairs={{0,2},{1,3},{2,4},{3,5},{4,6},{5,7},{6,8},{7,9},{8,10},{9,11},{10,... | collective-permute-start | bytes 6291464 | tf_op jit(solution)/shard_map/ppermute | solution.py:26
  9.5 92.9 %collective-permute-start.1 = (bf16[1024,1024]{1,0:T(8,128)(2,1)}, bf16[1024,1024]{1,0:T(8,128)(2,1)}, u32[]{:S(2)}, u32[]{:S(2)}) collective-permute-start(bf16[1024,1024]{1,0:T(8,128)(2,1)} %multiply_convert_fusion), channel_id=1, source_target_pairs={{0,1},{1,2},{2,3},{3,4},{4,5},{5,6},{6,7},{7,8},{8,9},{9,10},{10,1... | collective-permute-start | bytes 6291464 | tf_op jit(solution)/shard_map/ppermute | solution.py:26
  10.3 180.1 %collective-permute-start.2 = (bf16[1024,1024]{1,0:T(8,128)(2,1)}, bf16[1024,1024]{1,0:T(8,128)(2,1)}, u32[]{:S(2)}, u32[]{:S(2)}) collective-permute-start(bf16[1024,1024]{1,0:T(8,128)(2,1)} %multiply_convert_fusion), channel_id=1, source_target_pairs={{0,15},{1,0},{2,1},{3,2},{4,3},{5,4},{6,5},{7,6},{8,7},{9,8},{10,9... | collective-permute-start | bytes 6291464 | tf_op jit(solution)/shard_map/ppermute | solution.py:26
  14.3 179.2 %collective-permute-start.3 = (bf16[1024,1024]{1,0:T(8,128)(2,1)}, bf16[1024,1024]{1,0:T(8,128)(2,1)S(1)}, u32[]{:S(2)}, u32[]{:S(2)}) collective-permute-start(bf16[1024,1024]{1,0:T(8,128)(2,1)} %multiply_convert_fusion), channel_id=1, source_target_pairs={{0,14},{1,15},{2,0},{3,1},{4,2},{5,3},{6,4},{7,5},{8,6},{9,7},{10,... | collective-permute-start | bytes 6291464 | tf_op jit(solution)/shard_map/ppermute | solution.py:26
  14.9 90.7 %copy-start.4 = (f32[1024,1024]{1,0:T(8,128)S(1)}, f32[1024,1024]{1,0:T(8,128)}, u32[]{:S(2)}) copy-start(f32[1024,1024]{1,0:T(8,128)} %param.6) | copy-start | bytes 12582916
  205.0 26.2 %copy-start = (bf16[512,5120]{1,0:T(8,128)(2,1)}, bf16[512,5120]{1,0:T(8,128)(2,1)S(1)}, u32[]{:S(2)}) copy-start(bf16[512,5120]{1,0:T(8,128)(2,1)S(1)} %get-tuple-element.16) | copy-start | bytes 15728644
  205.0 12.0 %copy-start.5 = (f32[1024,64]{0,1:T(8,128)S(1)}, f32[1024,64]{0,1:T(8,128)}, u32[]{:S(2)}) copy-start(f32[1024,64]{0,1:T(8,128)} %param.8) | copy-start | bytes 786436
  217.0 17.6 %copy-start.1 = (bf16[512,5120]{1,0:T(8,128)(2,1)}, bf16[512,5120]{1,0:T(8,128)(2,1)S(1)}, u32[]{:S(2)}) copy-start(bf16[512,5120]{1,0:T(8,128)(2,1)S(1)} %get-tuple-element.14) | copy-start | bytes 15728644
  217.1 8.7 %collective-permute-start.4 = (bf16[1024,64]{0,1:T(8,128)(2,1)S(1)}, bf16[1024,64]{0,1:T(8,128)(2,1)S(1)}, u32[]{:S(2)}, u32[]{:S(2)}) collective-permute-start(bf16[1024,64]{0,1:T(8,128)(2,1)S(1)} %multiply_convert_fusion.1), channel_id=1, source_target_pairs={{0,2},{1,3},{2,4},{3,5},{4,6},{5,7},{6,8},{7,9},{8,10},{9,11},{10,... | collective-permute-start | bytes 393224 | tf_op jit(solution)/shard_map/ppermute | solution.py:26
  217.2 9.1 %collective-permute-start.5 = (bf16[1024,64]{0,1:T(8,128)(2,1)S(1)}, bf16[1024,64]{0,1:T(8,128)(2,1)S(1)}, u32[]{:S(2)}, u32[]{:S(2)}) collective-permute-start(bf16[1024,64]{0,1:T(8,128)(2,1)S(1)} %multiply_convert_fusion.1), channel_id=1, source_target_pairs={{0,1},{1,2},{2,3},{3,4},{4,5},{5,6},{6,7},{7,8},{8,9},{9,10},{10,1... | collective-permute-start | bytes 393224 | tf_op jit(solution)/shard_map/ppermute | solution.py:26
  217.2 9.1 %collective-permute-start.6 = (bf16[1024,64]{0,1:T(8,128)(2,1)S(1)}, bf16[1024,64]{0,1:T(8,128)(2,1)S(1)}, u32[]{:S(2)}, u32[]{:S(2)}) collective-permute-start(bf16[1024,64]{0,1:T(8,128)(2,1)S(1)} %multiply_convert_fusion.1), channel_id=1, source_target_pairs={{0,15},{1,0},{2,1},{3,2},{4,3},{5,4},{6,5},{7,6},{8,7},{9,8},{10,9... | collective-permute-start | bytes 393224 | tf_op jit(solution)/shard_map/ppermute | solution.py:26
  222.0 9.2 %collective-permute-start.7 = (bf16[1024,64]{0,1:T(8,128)(2,1)S(1)}, bf16[1024,64]{0,1:T(8,128)(2,1)S(1)}, u32[]{:S(2)}, u32[]{:S(2)}) collective-permute-start(bf16[1024,64]{0,1:T(8,128)(2,1)S(1)} %multiply_convert_fusion.1), channel_id=1, source_target_pairs={{0,14},{1,15},{2,0},{3,1},{4,2},{5,3},{6,4},{7,5},{8,6},{9,7},{10,... | collective-permute-start | bytes 393224 | tf_op jit(solution)/shard_map/ppermute | solution.py:26
  248.3 13.1 %all-to-all-start.1 = ((f32[8,1,4096]{2,1,0:T(1,128)}), f32[8,1,4096]{2,1,0:T(1,128)S(1)}, u32[]{:S(2)}, u32[]{:S(2)}) async-start(f32[8,1,4096]{2,1,0:T(1,128)} %reshape.76), calls=%async_computation.1 | async-start | bytes 262144 | tf_op jit(solution)/shard_map/all_to_all | solution.py:31
  274.7 18.0 %copy-start.2 = (bf16[512,5120]{1,0:T(8,128)(2,1)S(1)}, bf16[512,5120]{1,0:T(8,128)(2,1)}, u32[]{:S(2)}) copy-start(bf16[512,5120]{1,0:T(8,128)(2,1)} %copy-done.1) | copy-start | bytes 15728644
  275.2 7.9 %collective-permute-start.8 = (bf16[1024,64]{0,1:T(8,128)(2,1)S(1)}, bf16[1024,64]{0,1:T(8,128)(2,1)S(1)}, u32[]{:S(2)}, u32[]{:S(2)}) collective-permute-start(bf16[1024,64]{0,1:T(8,128)(2,1)S(1)} %fusion.3), channel_id=1, source_target_pairs={{0,2},{1,3},{2,4},{3,5},{4,6},{5,7},{6,8},{7,9},{8,10},{9,11},{10,... | collective-permute-start | bytes 393224 | tf_op jit(solution)/shard_map/ppermute | solution.py:26
  276.5 9.1 %collective-permute-start.9 = (bf16[1024,64]{0,1:T(8,128)(2,1)S(1)}, bf16[1024,64]{0,1:T(8,128)(2,1)S(1)}, u32[]{:S(2)}, u32[]{:S(2)}) collective-permute-start(bf16[1024,64]{0,1:T(8,128)(2,1)S(1)} %fusion.3), channel_id=1, source_target_pairs={{0,1},{1,2},{2,3},{3,4},{4,5},{5,6},{6,7},{7,8},{8,9},{9,10},{10,1... | collective-permute-start | bytes 393224 | tf_op jit(solution)/shard_map/ppermute | solution.py:26
  276.6 10.0 %collective-permute-start.10 = (bf16[1024,64]{0,1:T(8,128)(2,1)S(1)}, bf16[1024,64]{0,1:T(8,128)(2,1)S(1)}, u32[]{:S(2)}, u32[]{:S(2)}) collective-permute-start(bf16[1024,64]{0,1:T(8,128)(2,1)S(1)} %fusion.3), channel_id=1, source_target_pairs={{0,15},{1,0},{2,1},{3,2},{4,3},{5,4},{6,5},{7,6},{8,7},{9,8},{10,9... | collective-permute-start | bytes 393224 | tf_op jit(solution)/shard_map/ppermute | solution.py:26
  281.3 7.3 %collective-permute-start.11 = (bf16[1024,64]{0,1:T(8,128)(2,1)S(1)}, bf16[1024,64]{0,1:T(8,128)(2,1)S(1)}, u32[]{:S(2)}, u32[]{:S(2)}) collective-permute-start(bf16[1024,64]{0,1:T(8,128)(2,1)S(1)} %fusion.3), channel_id=1, source_target_pairs={{0,14},{1,15},{2,0},{3,1},{4,2},{5,3},{6,4},{7,5},{8,6},{9,7},{10,... | collective-permute-start | bytes 393224 | tf_op jit(solution)/shard_map/ppermute | solution.py:26
  333.5 7.9 %collective-permute-start.12 = (bf16[1024,64]{0,1:T(8,128)(2,1)S(1)}, bf16[1024,64]{0,1:T(8,128)(2,1)S(1)}, u32[]{:S(2)}, u32[]{:S(2)}) collective-permute-start(bf16[1024,64]{0,1:T(8,128)(2,1)S(1)} %fusion.4), channel_id=1, source_target_pairs={{0,2},{1,3},{2,4},{3,5},{4,6},{5,7},{6,8},{7,9},{8,10},{9,11},{10,... | collective-permute-start | bytes 393224 | tf_op jit(solution)/shard_map/ppermute | solution.py:26
  334.8 9.2 %collective-permute-start.13 = (bf16[1024,64]{0,1:T(8,128)(2,1)S(1)}, bf16[1024,64]{0,1:T(8,128)(2,1)S(1)}, u32[]{:S(2)}, u32[]{:S(2)}) collective-permute-start(bf16[1024,64]{0,1:T(8,128)(2,1)S(1)} %fusion.4), channel_id=1, source_target_pairs={{0,1},{1,2},{2,3},{3,4},{4,5},{5,6},{6,7},{7,8},{8,9},{9,10},{10,1... | collective-permute-start | bytes 393224 | tf_op jit(solution)/shard_map/ppermute | solution.py:26
  334.9 10.0 %collective-permute-start.14 = (bf16[1024,64]{0,1:T(8,128)(2,1)S(1)}, bf16[1024,64]{0,1:T(8,128)(2,1)S(1)}, u32[]{:S(2)}, u32[]{:S(2)}) collective-permute-start(bf16[1024,64]{0,1:T(8,128)(2,1)S(1)} %fusion.4), channel_id=1, source_target_pairs={{0,15},{1,0},{2,1},{3,2},{4,3},{5,4},{6,5},{7,6},{8,7},{9,8},{10,9... | collective-permute-start | bytes 393224 | tf_op jit(solution)/shard_map/ppermute | solution.py:26
  339.6 7.3 %collective-permute-start.15 = (bf16[1024,64]{0,1:T(8,128)(2,1)S(1)}, bf16[1024,64]{0,1:T(8,128)(2,1)S(1)}, u32[]{:S(2)}, u32[]{:S(2)}) collective-permute-start(bf16[1024,64]{0,1:T(8,128)(2,1)S(1)} %fusion.4), channel_id=1, source_target_pairs={{0,14},{1,15},{2,0},{3,1},{4,2},{5,3},{6,4},{7,5},{8,6},{9,7},{10,... | collective-permute-start | bytes 393224 | tf_op jit(solution)/shard_map/ppermute | solution.py:26
where the time goes:
time: 395 us
  waiting for transfers between devices  194 us (49%)
  blocking collectives  55.5 us (14%)
  other arithmetic  49.2 us (12%)
  matrix products  42.8 us (11%)
  starting transfers between devices  36.9 us (9%)
  local copies, waits for them, and re-layouts  16.1 us (4%)
    ppermute x16, waiting for transfers between devices, passed_along(): lax.ppermute(shard, axis, [(i, (i + by) % count) for i in range(count)])  188 us
    all_to_all x5, blocking collectives, sent_to_all(): lax.all_to_all(jnp.broadcast_to(shard[None], (count, *shard.shape)), axis...  55.5 us
    ppermute x16, starting transfers between devices, passed_along(): lax.ppermute(shard, axis, [(i, (i + by) % count) for i in range(count)])  29 us
    dot_general x2, matrix products, on_device(): lax.dot_general(own_blocks[member], point_rows, (((1,), (1,)), ((), ())),...  22 us
    another operation x9, other arithmetic, orthonormal(): factor = jnp.linalg.cholesky(gram_sum)  19.6 us
    dot_general x6, matrix products, on_device(): jnp.dot(tile_list[member], spread, preferred_element_type=jnp.float32)  17.7 us
    another operation x6, other arithmetic, orthonormal(): lax.linalg.triangular_solve(factor, image_rows, left_side=False, lower=Tr...  16.6 us
    unnamed x41, local copies, waits for them, and re-layouts  13.3 us
  transfers between devices with their start and end apart: 17, of which 15 were waited for; matrix products, arithmetic and copies ran while one was open for 3% of the time, Pallas kernels for 0%

commit v1 on v0

v1 whole, which is shorter than its diff:
```python
import functools
import math

import jax
import jax.numpy as jnp
from jax import lax
from jax.experimental import pallas as pl
from jax.experimental.pallas import tpu as pltpu
from jax.sharding import PartitionSpec as P

D = 1024
BS = 512
SLOTS = 12
K = 64
REACH = 2
ITERS = 3
BLK_DEV = 2
PTS = BS * BLK_DEV
SHARP = 8.0
EPSILON = 1e-06
CORES = 2
Z_CHIPS = 4
MESH = pl.DeviceIdType.MESH
BF16 = jnp.bfloat16
F32 = jnp.float32

CHUNKS = ((0, 256), (256, 256), (512, 256), (768, 256))
PARTIAL = BF16
HALF = PTS // 2
OO, PO, OP, NP, PN = range(5)
OWN, PREV, NEXT = range(3)


def split_hi_lo(x):
    hi = x.astype(BF16)
    return hi, (x - hi.astype(F32)).astype(BF16)


def gram_packed(image):
    hi, lo = split_hi_lo(image)
    both = jnp.concatenate([hi, lo], axis=0)
    full = lax.dot_general(both, both, (((1,), (1,)), ((), ())), preferred_element_type=F32)
    top = full[:K] + full[K:]
    gram = top[:, :K] + top[:, K:]
    return jnp.concatenate([gram[: K // 2], gram[K // 2 :]], axis=1)


def inverse_factor(packed):
    gram = jnp.concatenate([packed[:, :K], packed[:, K:]], axis=0)
    row_ids = lax.broadcasted_iota(jnp.int32, (K, K), 0)
    col_ids = lax.broadcasted_iota(jnp.int32, (K, K), 1)
    eye = jnp.where(row_ids == col_ids, 1.0, 0.0).astype(F32)
    work = jnp.concatenate([gram, eye], axis=1)
    in_group = lax.broadcasted_iota(jnp.int32, (8, 2 * K), 0)
    groups = [work[8 * g : 8 * g + 8] for g in range(K // 8)]
    for k in range(0, K, 2):
        first, r = divmod(k, 8)
        head = groups[first]
        one, two = head[r : r + 1], head[r + 1 : r + 2]
        a, b, d = one[:, k : k + 1], one[:, k + 1 : k + 2], two[:, k + 1 : k + 2]
        inv_a = 1.0 / a
        inv_det = 1.0 / (a * d - b * b)
        t_one = (d * inv_det) * one - (b * inv_det) * two
        t_two = (a * inv_det) * two - (b * inv_det) * one
        for g in range(first, K // 8):
            below = groups[g]
            new = below - below[:, k : k + 1] * t_one - below[:, k + 1 : k + 2] * t_two
            if g == first:
                second = two - (b * inv_a) * one
                new = jnp.where(in_group > r + 1, new, jnp.where(in_group == r + 1, second, below))
            groups[g] = new
    work = jnp.concatenate(groups, axis=0)
    pivots = jnp.sum(work[:, :K] * eye, axis=1, keepdims=True)
    return work[:, K:] * lax.rsqrt(pivots)


def apply_factor(inverse, image):
    mh, ml = split_hi_lo(inverse)
    zh, zl = split_hi_lo(image)
    left = jnp.concatenate([mh, mh, ml, ml], axis=1)
    right = jnp.concatenate([zh, zl, zh, zl], axis=0)
    return jnp.dot(left, right, preferred_element_type=F32)


def kernel(
    n_row, n_col,
    emb, ids, start, out,
    stage, normed, tiles, x_rows, own_mask, got_mask, masks, deg, got_deg,
    scaled, got_scaled, part, got_part, gram, got_gram,
    load_sem, x_sem, emb_send, emb_recv, mask_send, mask_recv, deg_send, deg_recv,
    vec_send, vec_recv, part_send, part_recv, gram_send, gram_recv,
):
    row, col = lax.axis_index("row"), lax.axis_index("col")
    prev = (row, lax.rem(col + n_col - 1, n_col))
    nxt = (row, lax.rem(col + 1, n_col))
    n_y, n_x = n_row // CORES, n_col // Z_CHIPS
    y, core = row // CORES, lax.rem(row, CORES)
    x, z = col // Z_CHIPS, lax.rem(col, Z_CHIPS)
    phases = [
        [(y * CORES + (1 - core), col)],
        [(lax.rem(y + k, n_y) * CORES + core, col) for k in range(1, n_y)],
        [(row, lax.rem(x + k, n_x) * Z_CHIPS + z) for k in range(1, n_x)],
        [(row, x * Z_CHIPS + lax.rem(z + k, Z_CHIPS)) for k in range(1, Z_CHIPS)],
    ]
    mirror = [[n - 1 - k for k in range(n)] for n in map(len, phases)]
    base = [sum(len(p) for p in phases[:i]) for i in range(len(phases))]

    loads = []
    for i, (begin, count) in enumerate(CHUNKS):
        load = pltpu.make_async_copy(
            emb.at[pl.ds(begin, count)], stage.at[pl.ds(begin, count)], load_sem.at[i]
        )
        load.start()
        loads.append(load)
    x_load = pltpu.make_async_copy(start, x_rows, x_sem)
    x_load.start()

    barrier = pltpu.get_barrier_semaphore()
    friends = [prev, nxt] + [d for p in phases for d in p]
    for friend in friends:
        pl.semaphore_signal(barrier, inc=1, device_id=friend, device_id_type=MESH)

    lane = lax.broadcasted_iota(jnp.int32, (BLK_DEV, 128), 1)
    holder = col + (lane >> 1) - REACH
    holder = jnp.where(holder < 0, holder + n_col, jnp.where(holder >= n_col, holder - n_col, holder))
    target = (row * n_col + holder) * BLK_DEV + (lane & 1)
    me = (row * n_col + col) * BLK_DEV + lax.broadcasted_iota(jnp.int32, (BLK_DEV, 128), 0)
    count_listed = jnp.zeros((BLK_DEV, 128), F32)
    for slot in range(SLOTS):
        named = ids[:, slot : slot + 1]
        hit = named == target
        if slot:
            hit = hit & (named != me)
        count_listed += jnp.where(hit, 1.0, 0.0)
    own_mask[...] = jnp.zeros((8, 128), F32)
    own_mask[0:BLK_DEV, :] = count_listed

    def normalize(begin, count):
        step = 32

        def some(i, carry):
            rows = pl.ds(begin + i * step, step)
            e = stage[rows, :]
            inv = lax.rsqrt(jnp.mean(e * e, axis=-1, keepdims=True) + EPSILON)
            normed[OWN, rows, :] = (e * inv).astype(BF16)
            return carry

        lax.fori_loop(0, count // step, some, 0)

    def remote(src, dst, send, recv, device):
        return pltpu.make_async_remote_copy(
            src_ref=src, dst_ref=dst, send_sem=send, recv_sem=recv, device_id=device, device_id_type=MESH
        )

    both = ((nxt, 0), (prev, 1))
    moving = [[], []]
    mask_copies = []
    for i, (begin, count) in enumerate(CHUNKS):
        loads[i].wait()
        normalize(begin, count)
        if i == 0:
            pl.semaphore_wait(barrier, len(friends))
            for device, side in both:
                copy = remote(own_mask, got_mask.at[side], mask_send.at[side], mask_recv.at[side], device)
                copy.start()
                mask_copies.append(copy)
        rows = pl.ds(begin, count)
        for device, side in both:
            copy = remote(
                normed.at[OWN, rows],
                normed.at[PREV + side, rows],
                emb_send.at[side, i],
                emb_recv.at[side, i],
                device,
            )
            copy.start()
            moving[side].append(copy)

    first_block = lax.broadcasted_iota(jnp.int32, (1, PTS), 1) < BS

    def spread_mask(tile, listing, candidate):
        for block in range(BLK_DEV):
            at = candidate + block
            masks[pl.ds(2 * tile + block, 1), :] = jnp.where(
                first_block, listing[0:1, at : at + 1], listing[1:2, at : at + 1]
            )

    def offset_at(offset):
        return (offset + REACH) * BLK_DEV

    left = {OO: OWN, PO: PREV, OP: OWN, NP: NEXT, PN: PREV}
    right = {OO: OWN, PO: OWN, OP: PREV, NP: PREV, PN: NEXT}

    def affinity(tile, r0, r_count, c0, c_count):
        a = normed[left[tile], pl.ds(r0, r_count), :]
        b = normed[right[tile], pl.ds(c0, c_count), :]
        product = lax.dot_general(a, b, (((1,), (1,)), ((), ())), preferred_element_type=F32)
        listed = masks[pl.ds(2 * tile + r0 // BS, 1), pl.ds(c0, c_count)]
        value = jnp.exp(product * (SHARP / D) - SHARP) * listed
        tiles[tile, pl.ds(r0, r_count), pl.ds(c0, c_count)] = value.astype(BF16)
        deg[right[tile], :, pl.ds(c0, c_count)] += jnp.sum(
            value.reshape(r_count // 8, 8, c_count), axis=0
        )

    deg[...] = jnp.zeros((3, 8, PTS), F32)
    mine = own_mask[...]
    spread_mask(OO, mine, offset_at(0))
    spread_mask(PO, mine, offset_at(-1))
    for begin, count in CHUNKS:
        affinity(OO, begin, count, 0, PTS)
    x_load.wait()
    x_cols = x_rows[...].T
    for copy in mask_copies:
        copy.wait()
    theirs = got_mask[0]
    spread_mask(OP, theirs, offset_at(1))
    spread_mask(NP, theirs, offset_at(2))
    spread_mask(PN, got_mask[1], offset_at(-2))

    for i, (begin, count) in enumerate(CHUNKS):
        moving[0][i].wait_recv()
        affinity(PO, begin, count, 0, PTS)
        for b0, n0 in CHUNKS:
            affinity(OP, b0, n0, begin, count)
        moving[1][i].wait_recv()
        end = begin + count
        affinity(NP, begin, count, 0, end)
        affinity(PN, begin, count, 0, end)
        for b0, n0 in CHUNKS[:i]:
            affinity(NP, b0, n0, begin, count)
            affinity(PN, b0, n0, begin, count)

    deg_copies = []
    for device, side in both:
        copy = remote(
            deg.at[NEXT - side], got_deg.at[side], deg_send.at[side], deg_recv.at[side], device
        )
        copy.start()
        deg_copies.append(copy)
    for copy in deg_copies:
        copy.wait_recv()
    degree = jnp.sum(deg[OWN] + got_deg[0] + got_deg[1], axis=0, keepdims=True)
    inv_root = lax.rsqrt(degree)

    pending = deg_copies + moving[0] + moving[1]
    sent_only = []

    def product(vectors, tile, c0, c_count):
        return jnp.dot(vectors, tiles[tile, :, pl.ds(c0, c_count)], preferred_element_type=F32)

    def reduce_send(it, phase, packed):
        gram[it, phase] = packed
        copies = []
        for k, device in enumerate(phases[phase]):
            slot = base[phase] + mirror[phase][k]
            copy = remote(
                gram.at[it, phase],
                got_gram.at[it, slot],
                gram_send.at[it, base[phase] + k],
                gram_recv.at[it, slot],
                device,
            )
            copy.start()
            copies.append(copy)
        sent_only.extend(copies)
        return copies

    def reduce_wait(it, phase, packed, copies):
        for copy in copies:
            copy.wait_recv()
        for k in range(len(phases[phase])):
            packed = packed + got_gram[it, base[phase] + k]
        return packed

    def no_beside(stage_index):
        return None

    def apply_affinity(it, vectors, beside):
        own_scaled = (vectors * inv_root).astype(BF16)
        scaled[it] = own_scaled
        copies = []
        for device, side in both:
            copy = remote(
                scaled.at[it], got_scaled.at[it, side], vec_send.at[it, side], vec_recv.at[it, side], device
            )
            copy.start()
            copies.append(copy)
        sent_only.extend(copies)
        beside(0)
        total = product(own_scaled, OO, 0, PTS)
        to_prev = product(own_scaled, OP, 0, PTS)
        beside(1)
        copies[0].wait_recv()
        copies[1].wait_recv()
        from_prev, from_next = got_scaled[it, 0], got_scaled[it, 1]
        part_copies = []
        for half in range(2):
            at = pl.ds(half * HALF, HALF)
            for device, side in both:
                if side == 0:
                    piece = product(from_prev, PN, half * HALF, HALF)
                else:
                    piece = to_prev[:, half * HALF : (half + 1) * HALF]
                    piece = piece + product(from_next, NP, half * HALF, HALF)
                part[it, side, half] = piece.astype(PARTIAL)
                copy = remote(
                    part.at[it, side, half],
                    got_part.at[it, side, half],
                    part_send.at[it, side, half],
                    part_recv.at[it, side, half],
                    device,
                )
                copy.start()
                part_copies.append(copy)
        sent_only.extend(part_copies)
        beside(2)
        total = total + product(from_prev, PO, 0, PTS)
        beside(3)
        for copy in part_copies:
            copy.wait_recv()
        halves = [
            got_part[it, 0, half].astype(F32) + got_part[it, 1, half].astype(F32) for half in range(2)
        ]
        return (total + jnp.concatenate(halves, axis=1)) * inv_root

    scale = math.sqrt(n_row * n_col * PTS)
    image = apply_affinity(0, x_cols, no_beside)
    for it in range(1, ITERS):
        state = {}

        def beside(stage_index):
            if stage_index == 0:
                state["sum"] = gram_packed(image)
            else:
                state["sum"] = reduce_wait(it - 1, stage_index - 1, state["sum"], state["copies"])
            if stage_index < len(phases):
                state["copies"] = reduce_send(it - 1, stage_index, state["sum"])

        following = apply_affinity(it, image, beside)
        beside(4)
        factor = inverse_factor(state["sum"]) * scale
        image = apply_factor(factor, following)

    packed = gram_packed(image)
    for phase in range(len(phases)):
        copies = reduce_send(ITERS - 1, phase, packed)
        packed = reduce_wait(ITERS - 1, phase, packed, copies)
    result = apply_factor(inverse_factor(packed) * scale, image)
    out[...] = result.T

    for copy in pending + sent_only:
        copy.wait_send()


def on_device(n_row, n_col, embeddings, neighbour_ids, start_vectors):
    sums = 1 + (n_row // CORES - 1) + (n_col // Z_CHIPS - 1) + (Z_CHIPS - 1)
    n_chunks = len(CHUNKS)
    return pl.pallas_call(
        functools.partial(kernel, n_row, n_col),
        out_shape=jax.ShapeDtypeStruct((PTS, K), F32),
        in_specs=[
            pl.BlockSpec(memory_space=pl.ANY),
            pl.BlockSpec(memory_space=pltpu.VMEM),
            pl.BlockSpec(memory_space=pl.ANY),
        ],
        out_specs=pl.BlockSpec(memory_space=pltpu.VMEM),
        scratch_shapes=[
            pltpu.VMEM((PTS, D), F32),
            pltpu.VMEM((3, PTS, D), BF16),
            pltpu.VMEM((5, PTS, PTS), BF16),
            pltpu.VMEM((PTS, K), F32),
            pltpu.VMEM((8, 128), F32),
            pltpu.VMEM((2, 8, 128), F32),
            pltpu.VMEM((16, PTS), F32),
            pltpu.VMEM((3, 8, PTS), F32),
            pltpu.VMEM((2, 8, PTS), F32),
            pltpu.VMEM((ITERS, K, PTS), BF16),
            pltpu.VMEM((ITERS, 2, K, PTS), BF16),
            pltpu.VMEM((ITERS, 2, 2, K, HALF), PARTIAL),
            pltpu.VMEM((ITERS, 2, 2, K, HALF), PARTIAL),
            pltpu.VMEM((ITERS, 4, K // 2, 2 * K), F32),
            pltpu.VMEM((ITERS, sums, K // 2, 2 * K), F32),
            pltpu.SemaphoreType.DMA((n_chunks,)),
            pltpu.SemaphoreType.DMA,
            pltpu.SemaphoreType.DMA((2, n_chunks)),
            pltpu.SemaphoreType.DMA((2, n_chunks)),
            pltpu.SemaphoreType.DMA((2,)),
            pltpu.SemaphoreType.DMA((2,)),
            pltpu.SemaphoreType.DMA((2,)),
            pltpu.SemaphoreType.DMA((2,)),
            pltpu.SemaphoreType.DMA((ITERS, 2)),
            pltpu.SemaphoreType.DMA((ITERS, 2)),
            pltpu.SemaphoreType.DMA((ITERS, 2, 2)),
            pltpu.SemaphoreType.DMA((ITERS, 2, 2)),
            pltpu.SemaphoreType.DMA((ITERS, sums)),
            pltpu.SemaphoreType.DMA((ITERS, sums)),
        ],
        compiler_params=pltpu.CompilerParams(
            collective_id=0, has_side_effects=True, vmem_limit_bytes=48 * 2**20
        ),
    )(embeddings, neighbour_ids, start_vectors)


def solution(mesh):
    split = P(("row", "col"), None)
    return jax.shard_map(
        functools.partial(on_device, mesh.shape["row"], mesh.shape["col"]),
        mesh=mesh,
        in_specs=(split, split, split),
        out_specs=split,
        check_vma=False,
    )
```

time: 395 us -> 147 us (0.37)
  waiting for transfers between devices: 194 us -> 0 us
  Pallas kernels: 0 us -> 141 us
  blocking collectives: 55.5 us -> 0 us
  other arithmetic: 49.2 us -> 0 us
  matrix products: 42.8 us -> 0 us
  starting transfers between devices: 36.9 us -> 0 us
  local copies, waits for them, and re-layouts: 16.1 us -> 4.89 us
    ppermute x16 -> x0, waiting for transfers between devices: 188 us -> none  [passed_along(): lax.ppermute(shard, axis, [(i, (i + by) % count) for i in range(count)])]
    pallas_call x0 -> x1, Pallas kernels: none -> 141 us  [on_device(): pl.pallas_call(functools.partial(kernel, n_row, n_col), out_shape=jax.Sha...]
    all_to_all x5 -> x0, blocking collectives: 55.5 us -> none  [sent_to_all(): lax.all_to_all(jnp.broadcast_to(shard[None], (count, *shard.shape)), axis...]
    dot_general x11 -> x0, matrix products: 40.8 us -> none  [the longest x2 22 us: on_device(): lax.dot_general(own_blocks[member], point_rows, (((1,), (1,)), ((), ())),...]
    another operation x15 -> x0, other arithmetic: 36.2 us -> none  [the longest x9 19.6 us: orthonormal(): factor = jnp.linalg.cholesky(gram_sum)]
    ppermute x16 -> x0, starting transfers between devices: 29 us -> none  [passed_along(): lax.ppermute(shard, axis, [(i, (i + by) % count) for i in range(count)])]
    unnamed x41 -> x5, local copies, waits for them, and re-layouts: 13.3 us -> 4.01 us
    all_to_all x1 -> x0, starting transfers between devices: 7.87 us -> none  [sent_to_all(): lax.all_to_all(jnp.broadcast_to(shard[None], (count, *shard.shape)), axis...]
  transfers between devices with their start and end apart: 17 -> 0, of which waited for: 15 -> 0; matrix products, arithmetic and copies ran while one was open for 3% -> 0% of each run, Pallas kernels for 0% -> 0%
where the time goes in v1:
time: 147 us; the launch traced here: 146 us
  Pallas kernels  141 us (96%)
  local copies, waits for them, and re-layouts  4.89 us (3%)
    pallas_call x1, Pallas kernels, on_device(): pl.pallas_call(functools.partial(kernel, n_row, n_col), out_shape=jax.Sha...  141 us
    unnamed x5, local copies, waits for them, and re-layouts  4.01 us

profile of v1, /device:TPU:1, one launch (start us, length us, event | category | flops | bytes accessed | tf_op | source)
XLA Modules:
  0.0 146.2 jit_solution(13277519412625796949)
XLA Ops:
  0.0 1.1 copy.4.start
  1.2 0.0 copy-start
  1.2 2.2 %copy-done = f32[1024,1024]{1,0:T(8,128)S(1)} copy-done((f32[1024,1024]{1,0:T(8,128)S(1)}, f32[1024,1024]{1,0:T(8,128)}, u32[]{:S(2)}) %copy-start) | copy-done | bytes 4194328
  3.3 0.0 copy-start.1
  3.3 0.7 copy-done.1
  4.0 141.2 %shard_map.37 = f32[1024,64]{1,0:T(8,128)S(1)} custom-call(f32[1024,1024]{1,0:T(8,128)S(1)} %copy-done, s32[2,12]{1,0:T(2,128)S(1)} %copy-done.1, f32[1024,64]{1,0:T(8,128)S(1)} %copy.4.start), custom_call_target="tpu_custom_call" | custom-call | tf_op jit(solution)/shard_map/pallas_call | solution.py:358
  145.3 0.9 copy.5
Async XLA Ops:
  1.2 2.2 %copy-start = (f32[1024,1024]{1,0:T(8,128)S(1)}, f32[1024,1024]{1,0:T(8,128)}, u32[]{:S(2)}) copy-start(f32[1024,1024]{1,0:T(8,128)} %emb.1) | copy-start | bytes 12582916
  3.3 0.7 copy-start.1

commit v2 on v1

--- a/solution.py
+++ b/solution.py
@@ -24,7 +24,7 @@
 BF16 = jnp.bfloat16
 F32 = jnp.float32
 
-CHUNKS = ((0, 256), (256, 256), (512, 256), (768, 256))
+CHUNKS = ((0, 256), (256, 256), (512, 256), (768, 128), (896, 128))
 PARTIAL = BF16
 HALF = PTS // 2
 OO, PO, OP, NP, PN = range(5)
@@ -84,8 +84,8 @@
 
 def kernel(
     n_row, n_col,
-    emb, ids, start, out,
-    stage, normed, tiles, x_rows, own_mask, got_mask, masks, deg, got_deg,
+    emb, ids_given, start, out,
+    stage, normed, tiles, x_cols, ids, own_mask, got_mask, masks, deg, got_deg,
     scaled, got_scaled, part, got_part, gram, got_gram,
     load_sem, x_sem, emb_send, emb_recv, mask_send, mask_recv, deg_send, deg_recv,
     vec_send, vec_recv, part_send, part_recv, gram_send, gram_recv,
@@ -96,14 +96,19 @@
     n_y, n_x = n_row // CORES, n_col // Z_CHIPS
     y, core = row // CORES, lax.rem(row, CORES)
     x, z = col // Z_CHIPS, lax.rem(col, Z_CHIPS)
+    steps = [
+        [(a, b) for a in range(n_y) for b in range(CORES) if a or b],
+        [(a, b) for a in range(n_x) for b in range(Z_CHIPS) if a or b],
+    ]
     phases = [
-        [(y * CORES + (1 - core), col)],
-        [(lax.rem(y + k, n_y) * CORES + core, col) for k in range(1, n_y)],
-        [(row, lax.rem(x + k, n_x) * Z_CHIPS + z) for k in range(1, n_x)],
-        [(row, x * Z_CHIPS + lax.rem(z + k, Z_CHIPS)) for k in range(1, Z_CHIPS)],
+        [(lax.rem(y + a, n_y) * CORES + lax.rem(core + b, CORES), col) for a, b in steps[0]],
+        [(row, lax.rem(x + a, n_x) * Z_CHIPS + lax.rem(z + b, Z_CHIPS)) for a, b in steps[1]],
     ]
-    mirror = [[n - 1 - k for k in range(n)] for n in map(len, phases)]
-    base = [sum(len(p) for p in phases[:i]) for i in range(len(phases))]
+    mirror = [
+        [steps[0].index((-a % n_y, -b % CORES)) for a, b in steps[0]],
+        [steps[1].index((-a % n_x, -b % Z_CHIPS)) for a, b in steps[1]],
+    ]
+    base = [0, len(steps[0])]
 
     loads = []
     for i, (begin, count) in enumerate(CHUNKS):
@@ -112,11 +117,13 @@
         )
         load.start()
         loads.append(load)
-    x_load = pltpu.make_async_copy(start, x_rows, x_sem)
+    x_load = pltpu.make_async_copy(start, x_cols, x_sem.at[0])
     x_load.start()
+    ids_load = pltpu.make_async_copy(ids_given, ids, x_sem.at[1])
+    ids_load.start()
 
     barrier = pltpu.get_barrier_semaphore()
-    friends = [prev, nxt] + [d for p in phases for d in p]
+    friends = [d for p in phases for d in p]
     for friend in friends:
         pl.semaphore_signal(barrier, inc=1, device_id=friend, device_id_type=MESH)
 
@@ -125,6 +132,7 @@
     holder = jnp.where(holder < 0, holder + n_col, jnp.where(holder >= n_col, holder - n_col, holder))
     target = (row * n_col + holder) * BLK_DEV + (lane & 1)
     me = (row * n_col + col) * BLK_DEV + lax.broadcasted_iota(jnp.int32, (BLK_DEV, 128), 0)
+    ids_load.wait()
     count_listed = jnp.zeros((BLK_DEV, 128), F32)
     for slot in range(SLOTS):
         named = ids[:, slot : slot + 1]
@@ -209,7 +217,6 @@
     for begin, count in CHUNKS:
         affinity(OO, begin, count, 0, PTS)
     x_load.wait()
-    x_cols = x_rows[...].T
     for copy in mask_copies:
         copy.wait()
     theirs = got_mask[0]
@@ -276,6 +283,7 @@
         return None
 
     def apply_affinity(it, vectors, beside):
+        beside(0)
         own_scaled = (vectors * inv_root).astype(BF16)
         scaled[it] = own_scaled
         copies = []
@@ -286,7 +294,6 @@
             copy.start()
             copies.append(copy)
         sent_only.extend(copies)
-        beside(0)
         total = product(own_scaled, OO, 0, PTS)
         to_prev = product(own_scaled, OP, 0, PTS)
         beside(1)
@@ -313,9 +320,8 @@
                 copy.start()
                 part_copies.append(copy)
         sent_only.extend(part_copies)
+        total = total + product(from_prev, PO, 0, PTS)
         beside(2)
-        total = total + product(from_prev, PO, 0, PTS)
-        beside(3)
         for copy in part_copies:
             copy.wait_recv()
         halves = [
@@ -324,7 +330,7 @@
         return (total + jnp.concatenate(halves, axis=1)) * inv_root
 
     scale = math.sqrt(n_row * n_col * PTS)
-    image = apply_affinity(0, x_cols, no_beside)
+    image = apply_affinity(0, x_cols[...], no_beside)
     for it in range(1, ITERS):
         state = {}
 
@@ -335,32 +341,32 @@
                 state["sum"] = reduce_wait(it - 1, stage_index - 1, state["sum"], state["copies"])
             if stage_index < len(phases):
                 state["copies"] = reduce_send(it - 1, stage_index, state["sum"])
+            else:
+                state["factor"] = inverse_factor(state["sum"]) * scale
 
         following = apply_affinity(it, image, beside)
-        beside(4)
-        factor = inverse_factor(state["sum"]) * scale
-        image = apply_factor(factor, following)
+        image = apply_factor(state["factor"], following)
 
     packed = gram_packed(image)
     for phase in range(len(phases)):
         copies = reduce_send(ITERS - 1, phase, packed)
         packed = reduce_wait(ITERS - 1, phase, packed, copies)
     result = apply_factor(inverse_factor(packed) * scale, image)
-    out[...] = result.T
+    out[...] = result
 
     for copy in pending + sent_only:
         copy.wait_send()
 
 
 def on_device(n_row, n_col, embeddings, neighbour_ids, start_vectors):
-    sums = 1 + (n_row // CORES - 1) + (n_col // Z_CHIPS - 1) + (Z_CHIPS - 1)
+    sums = n_row - 1 + n_col - 1
     n_chunks = len(CHUNKS)
     return pl.pallas_call(
         functools.partial(kernel, n_row, n_col),
-        out_shape=jax.ShapeDtypeStruct((PTS, K), F32),
+        out_shape=jax.ShapeDtypeStruct((K, PTS), F32),
         in_specs=[
             pl.BlockSpec(memory_space=pl.ANY),
-            pl.BlockSpec(memory_space=pltpu.VMEM),
+            pl.BlockSpec(memory_space=pl.ANY),
             pl.BlockSpec(memory_space=pl.ANY),
         ],
         out_specs=pl.BlockSpec(memory_space=pltpu.VMEM),
@@ -368,7 +374,8 @@
             pltpu.VMEM((PTS, D), F32),
             pltpu.VMEM((3, PTS, D), BF16),
             pltpu.VMEM((5, PTS, PTS), BF16),
-            pltpu.VMEM((PTS, K), F32),
+            pltpu.VMEM((K, PTS), F32),
+            pltpu.VMEM((BLK_DEV, SLOTS), jnp.int32),
             pltpu.VMEM((8, 128), F32),
             pltpu.VMEM((2, 8, 128), F32),
             pltpu.VMEM((16, PTS), F32),
@@ -378,10 +385,10 @@
             pltpu.VMEM((ITERS, 2, K, PTS), BF16),
             pltpu.VMEM((ITERS, 2, 2, K, HALF), PARTIAL),
             pltpu.VMEM((ITERS, 2, 2, K, HALF), PARTIAL),
-            pltpu.VMEM((ITERS, 4, K // 2, 2 * K), F32),
+            pltpu.VMEM((ITERS, 2, K // 2, 2 * K), F32),
             pltpu.VMEM((ITERS, sums, K // 2, 2 * K), F32),
             pltpu.SemaphoreType.DMA((n_chunks,)),
-            pltpu.SemaphoreType.DMA,
+            pltpu.SemaphoreType.DMA((2,)),
             pltpu.SemaphoreType.DMA((2, n_chunks)),
             pltpu.SemaphoreType.DMA((2, n_chunks)),
             pltpu.SemaphoreType.DMA((2,)),
@@ -396,9 +403,9 @@
             pltpu.SemaphoreType.DMA((ITERS, sums)),
         ],
         compiler_params=pltpu.CompilerParams(
-            collective_id=0, has_side_effects=True, vmem_limit_bytes=48 * 2**20
+            collective_id=0, has_side_effects=True, vmem_limit_bytes=63 * 2**20
         ),
-    )(embeddings, neighbour_ids, start_vectors)
+    )(embeddings, neighbour_ids, start_vectors.T).T
 
 
 def solution(mesh):

time: 147 us -> 139 us (0.946)
  Pallas kernels: 141 us -> 137 us
  local copies, waits for them, and re-layouts: 4.89 us -> 1.67 us
    pallas_call x1, Pallas kernels: 141 us -> 137 us  [on_device(): pl.pallas_call(functools.partial(kernel, n_row, n_col), out_shape=jax.Sha...]
    unnamed x5 -> x1, local copies, waits for them, and re-layouts: 4.01 us -> 1.67 us
where the time goes in v2:
time: 139 us
  Pallas kernels  137 us (99%)
  local copies, waits for them, and re-layouts  1.67 us (1%)
    pallas_call x1, Pallas kernels, on_device(): pl.pallas_call(functools.partial(kernel, n_row, n_col), out_shape=jax.Sha...  137 us

profile of v2, /device:TPU:1, one launch (start us, length us, event | category | flops | bytes accessed | tf_op | source)
XLA Modules:
  0.0 138.7 jit_solution(7734496684740797535)
XLA Ops:
  0.0 137.0 %shard_map.37 = f32[64,1024]{1,0:T(8,128)} custom-call(f32[1024,1024]{1,0:T(8,128)} %emb.1, s32[2,12]{1,0:T(2,128)} %ids_given.1, f32[64,1024]{1,0:T(8,128)} %bitcast.3), custom_call_target="tpu_custom_call" | custom-call | tf_op jit(solution)/shard_map/pallas_call | solution.py:364
  137.0 1.7 %copy.5 = f32[1024,64]{0,1:T(8,128)} copy(f32[1024,64]{0,1:T(8,128)} %bitcast.2) | data formatting | bytes 524288

commit v3 on v2

--- a/solution.py
+++ b/solution.py
@@ -53,25 +53,60 @@
     work = jnp.concatenate([gram, eye], axis=1)
     in_group = lax.broadcasted_iota(jnp.int32, (8, 2 * K), 0)
     groups = [work[8 * g : 8 * g + 8] for g in range(K // 8)]
-    for k in range(0, K, 2):
+
+    def wide(value):
+        return jnp.broadcast_to(value, (8, 2 * K))
+
+    for k in range(0, K, 4):
         first, r = divmod(k, 8)
         head = groups[first]
-        one, two = head[r : r + 1], head[r + 1 : r + 2]
-        a, b, d = one[:, k : k + 1], one[:, k + 1 : k + 2], two[:, k + 1 : k + 2]
+        rows = [wide(head[r + i : r + i + 1]) for i in range(4)]
+        p = {
+            (i, j): wide(head[r + i : r + i + 1, k + j : k + j + 1])
+            for i in range(4)
+            for j in range(i, 4)
+        }
+        columns = [[wide(group[:, k + i : k + i + 1]) for i in range(4)] for group in groups[first:]]
+        a, b, d = p[0, 0], p[0, 1], p[1, 1]
         inv_a = 1.0 / a
         inv_det = 1.0 / (a * d - b * b)
-        t_one = (d * inv_det) * one - (b * inv_det) * two
-        t_two = (a * inv_det) * two - (b * inv_det) * one
+        d_, b_, a_ = d * inv_det, b * inv_det, a * inv_det
+        w = {j: (d_ * p[0, j] - b_ * p[1, j], a_ * p[1, j] - b_ * p[0, j]) for j in (2, 3)}
+        u0 = d_ * rows[0] - b_ * rows[1]
+        u1 = a_ * rows[1] - b_ * rows[0]
+        s22 = p[2, 2] - w[2][0] * p[0, 2] - w[2][1] * p[1, 2]
+        s23 = p[2, 3] - w[2][0] * p[0, 3] - w[2][1] * p[1, 3]
+        s33 = p[3, 3] - w[3][0] * p[0, 3] - w[3][1] * p[1, 3]
+        inv_s22 = 1.0 / s22
+        inv_rest = 1.0 / (s22 * s33 - s23 * s23)
+        s2 = rows[2] - p[0, 2] * u0 - p[1, 2] * u1
+        s3 = rows[3] - p[0, 3] * u0 - p[1, 3] * u1
+        t2 = (s33 * inv_rest) * s2 - (s23 * inv_rest) * s3
+        t3 = (s22 * inv_rest) * s3 - (s23 * inv_rest) * s2
+        t0 = u0 - w[2][0] * t2 - w[3][0] * t3
+        t1 = u1 - w[2][1] * t2 - w[3][1] * t3
         for g in range(first, K // 8):
+            c = columns[g - first]
             below = groups[g]
-            new = below - below[:, k : k + 1] * t_one - below[:, k + 1 : k + 2] * t_two
+            new = below - (c[0] * t0 + c[1] * t1) - (c[2] * t2 + c[3] * t3)
             if g == first:
-                second = two - (b * inv_a) * one
-                new = jnp.where(in_group > r + 1, new, jnp.where(in_group == r + 1, second, below))
+                second = rows[1] - (b * inv_a) * rows[0]
+                fourth = s3 - (s23 * inv_s22) * s2
+                kept = jnp.where(in_group == r + 2, s2, jnp.where(in_group == r + 3, fourth, below))
+                kept = jnp.where(in_group == r + 1, second, kept)
+                new = jnp.where(in_group > r + 3, new, kept)
             groups[g] = new
     work = jnp.concatenate(groups, axis=0)
     pivots = jnp.sum(work[:, :K] * eye, axis=1, keepdims=True)
     return work[:, K:] * lax.rsqrt(pivots)
+
+
+def folded(row):
+    return jnp.concatenate([row[:, 128 * g : 128 * g + 128] for g in range(PTS // 128)], axis=0)
+
+
+def unfolded(tile):
+    return jnp.concatenate([tile[g : g + 1] for g in range(PTS // 128)], axis=1)
 
 
 def apply_factor(inverse, image):
@@ -85,9 +120,10 @@
 def kernel(
     n_row, n_col,
     emb, ids_given, start, out,
-    stage, normed, tiles, x_cols, ids, own_mask, got_mask, masks, deg, got_deg,
+    stage, normed, tiles, x_cols, ids, own_mask, got_mask, masks, deg, deg_sum, near_deg, far_deg,
+    x_half, got_x, factors,
     scaled, got_scaled, part, got_part, gram, got_gram,
-    load_sem, x_sem, emb_send, emb_recv, mask_send, mask_recv, deg_send, deg_recv,
+    load_sem, x_sem, emb_send, emb_recv, mask_send, mask_recv, deg_send, deg_recv, start_send, start_recv,
     vec_send, vec_recv, part_send, part_recv, gram_send, gram_recv,
 ):
     row, col = lax.axis_index("row"), lax.axis_index("col")
@@ -162,6 +198,7 @@
 
     both = ((nxt, 0), (prev, 1))
     moving = [[], []]
+    start_copies = []
     mask_copies = []
     for i, (begin, count) in enumerate(CHUNKS):
         loads[i].wait()
@@ -183,6 +220,13 @@
             )
             copy.start()
             moving[side].append(copy)
+        if i == 0:
+            x_load.wait()
+            x_half[...] = x_cols[...].astype(BF16)
+            for device, side in both:
+                copy = remote(x_half, got_x.at[side], start_send.at[side], start_recv.at[side], device)
+                copy.start()
+                start_copies.append(copy)
 
     first_block = lax.broadcasted_iota(jnp.int32, (1, PTS), 1) < BS
 
@@ -203,8 +247,13 @@
         a = normed[left[tile], pl.ds(r0, r_count), :]
         b = normed[right[tile], pl.ds(c0, c_count), :]
         product = lax.dot_general(a, b, (((1,), (1,)), ((), ())), preferred_element_type=F32)
-        listed = masks[pl.ds(2 * tile + r0 // BS, 1), pl.ds(c0, c_count)]
-        value = jnp.exp(product * (SHARP / D) - SHARP) * listed
+        value = jnp.exp(product * (SHARP / D) - SHARP)
+        lists = [masks[pl.ds(2 * tile + block, 1), pl.ds(c0, c_count)] for block in range(BLK_DEV)]
+        if r0 < BS < r0 + r_count:
+            above = BS - r0
+            value = jnp.concatenate([value[:above] * lists[0], value[above:] * lists[1]], axis=0)
+        else:
+            value = value * lists[r0 // BS]
         tiles[tile, pl.ds(r0, r_count), pl.ds(c0, c_count)] = value.astype(BF16)
         deg[right[tile], :, pl.ds(c0, c_count)] += jnp.sum(
             value.reshape(r_count // 8, 8, c_count), axis=0
@@ -216,7 +265,6 @@
     spread_mask(PO, mine, offset_at(-1))
     for begin, count in CHUNKS:
         affinity(OO, begin, count, 0, PTS)
-    x_load.wait()
     for copy in mask_copies:
         copy.wait()
     theirs = got_mask[0]
@@ -227,29 +275,34 @@
     for i, (begin, count) in enumerate(CHUNKS):
         moving[0][i].wait_recv()
         affinity(PO, begin, count, 0, PTS)
-        for b0, n0 in CHUNKS:
-            affinity(OP, b0, n0, begin, count)
+        affinity(OP, 0, PTS, begin, count)
         moving[1][i].wait_recv()
         end = begin + count
         affinity(NP, begin, count, 0, end)
         affinity(PN, begin, count, 0, end)
-        for b0, n0 in CHUNKS[:i]:
-            affinity(NP, b0, n0, begin, count)
-            affinity(PN, b0, n0, begin, count)
-
-    deg_copies = []
-    for device, side in both:
-        copy = remote(
-            deg.at[NEXT - side], got_deg.at[side], deg_send.at[side], deg_recv.at[side], device
-        )
+        if begin:
+            affinity(NP, 0, begin, begin, count)
+            affinity(PN, 0, begin, begin, count)
+
+    for place, where in enumerate((PREV, OWN, NEXT)):
+        deg_sum[place] = folded(jnp.sum(deg[where], axis=0, keepdims=True))
+    far_prev = (row, lax.rem(col + n_col - 2, n_col))
+    far_next = (row, lax.rem(col + 2, n_col))
+    deg_copies = [
+        remote(deg_sum.at[pl.ds(1, 2)], near_deg.at[0], deg_send.at[0], deg_recv.at[0], nxt),
+        remote(deg_sum.at[pl.ds(0, 2)], near_deg.at[1], deg_send.at[1], deg_recv.at[1], prev),
+        remote(deg_sum.at[2], far_deg.at[0], deg_send.at[2], deg_recv.at[2], far_next),
+        remote(deg_sum.at[0], far_deg.at[1], deg_send.at[3], deg_recv.at[3], far_prev),
+    ]
+    for copy in deg_copies:
         copy.start()
-        deg_copies.append(copy)
-    for copy in deg_copies:
+    for copy in start_copies + deg_copies:
         copy.wait_recv()
-    degree = jnp.sum(deg[OWN] + got_deg[0] + got_deg[1], axis=0, keepdims=True)
-    inv_root = lax.rsqrt(degree)
-
-    pending = deg_copies + moving[0] + moving[1]
+    inv_root = unfolded(lax.rsqrt(deg_sum[1] + near_deg[0, 1] + near_deg[1, 0]))
+    inv_prev = unfolded(lax.rsqrt(deg_sum[0] + near_deg[0, 0] + far_deg[0]))
+    inv_next = unfolded(lax.rsqrt(deg_sum[2] + near_deg[1, 1] + far_deg[1]))
+
+    pending = deg_copies + start_copies + moving[0] + moving[1]
     sent_only = []
 
     def product(vectors, tile, c0, c_count):
@@ -282,24 +335,35 @@
     def no_beside(stage_index):
         return None
 
+    def scaled_start(side, inverse):
+        return (got_x[side].astype(F32) * inverse).astype(BF16)
+
     def apply_affinity(it, vectors, beside):
         beside(0)
         own_scaled = (vectors * inv_root).astype(BF16)
-        scaled[it] = own_scaled
         copies = []
-        for device, side in both:
-            copy = remote(
-                scaled.at[it], got_scaled.at[it, side], vec_send.at[it, side], vec_recv.at[it, side], device
-            )
-            copy.start()
-            copies.append(copy)
-        sent_only.extend(copies)
+        if it:
+            scaled[it - 1] = own_scaled
+            for device, side in both:
+                copy = remote(
+                    scaled.at[it - 1],
+                    got_scaled.at[it - 1, side],
+                    vec_send.at[it - 1, side],
+                    vec_recv.at[it - 1, side],
+                    device,
+                )
+                copy.start()
+                copies.append(copy)
+            sent_only.extend(copies)
         total = product(own_scaled, OO, 0, PTS)
         to_prev = product(own_scaled, OP, 0, PTS)
         beside(1)
-        copies[0].wait_recv()
-        copies[1].wait_recv()
-        from_prev, from_next = got_scaled[it, 0], got_scaled[it, 1]
+        if it:
+            for copy in copies:
+                copy.wait_recv()
+            from_prev, from_next = got_scaled[it - 1, 0], got_scaled[it - 1, 1]
+        else:
+            from_prev, from_next = scaled_start(0, inv_prev), scaled_start(1, inv_next)
         part_copies = []
         for half in range(2):
             at = pl.ds(half * HALF, HALF)
@@ -342,10 +406,10 @@
             if stage_index < len(phases):
                 state["copies"] = reduce_send(it - 1, stage_index, state["sum"])
             else:
-                state["factor"] = inverse_factor(state["sum"]) * scale
+                factors[it - 1] = inverse_factor(state["sum"]) * scale
 
         following = apply_affinity(it, image, beside)
-        image = apply_factor(state["factor"], following)
+        image = apply_factor(factors[it - 1], following)
 
     packed = gram_packed(image)
     for phase in range(len(phases)):
@@ -380,9 +444,14 @@
             pltpu.VMEM((2, 8, 128), F32),
             pltpu.VMEM((16, PTS), F32),
             pltpu.VMEM((3, 8, PTS), F32),
-            pltpu.VMEM((2, 8, PTS), F32),
-            pltpu.VMEM((ITERS, K, PTS), BF16),
-            pltpu.VMEM((ITERS, 2, K, PTS), BF16),
+            pltpu.VMEM((3, 8, 128), F32),
+            pltpu.VMEM((2, 2, 8, 128), F32),
+            pltpu.VMEM((2, 8, 128), F32),
+            pltpu.VMEM((K, PTS), BF16),
+            pltpu.VMEM((2, K, PTS), BF16),
+            pltpu.VMEM((ITERS - 1, K, K), F32),
+            pltpu.VMEM((ITERS - 1, K, PTS), BF16),
+            pltpu.VMEM((ITERS - 1, 2, K, PTS), BF16),
             pltpu.VMEM((ITERS, 2, 2, K, HALF), PARTIAL),
             pltpu.VMEM((ITERS, 2, 2, K, HALF), PARTIAL),
             pltpu.VMEM((ITERS, 2, K // 2, 2 * K), F32),
@@ -393,10 +462,12 @@
             pltpu.SemaphoreType.DMA((2, n_chunks)),
             pltpu.SemaphoreType.DMA((2,)),
             pltpu.SemaphoreType.DMA((2,)),
+            pltpu.SemaphoreType.DMA((4,)),
+            pltpu.SemaphoreType.DMA((4,)),
             pltpu.SemaphoreType.DMA((2,)),
             pltpu.SemaphoreType.DMA((2,)),
-            pltpu.SemaphoreType.DMA((ITERS, 2)),
-            pltpu.SemaphoreType.DMA((ITERS, 2)),
+            pltpu.SemaphoreType.DMA((ITERS - 1, 2)),
+            pltpu.SemaphoreType.DMA((ITERS - 1, 2)),
             pltpu.SemaphoreType.DMA((ITERS, 2, 2)),
             pltpu.SemaphoreType.DMA((ITERS, 2, 2)),
             pltpu.SemaphoreType.DMA((ITERS, sums)),

time: 139 us -> 123 us (0.88)
  Pallas kernels: 137 us -> 121 us
    pallas_call x1, Pallas kernels: 137 us -> 121 us  [on_device(): pl.pallas_call(functools.partial(kernel, n_row, n_col), out_shape=jax.Sha...]
where the time goes in v3:
time: 123 us; the launch traced here: 122 us
  Pallas kernels  121 us (98%)
  local copies, waits for them, and re-layouts  1.67 us (1%)
    pallas_call x1, Pallas kernels, on_device(): pl.pallas_call(functools.partial(kernel, n_row, n_col), out_shape=jax.Sha...  121 us

profile of v3, /device:TPU:1, one launch (start us, length us, event | category | flops | bytes accessed | tf_op | source)
XLA Modules:
  0.0 122.4 jit_solution(6596453370636731316)
XLA Ops:
  0.0 120.8 %shard_map.37 = f32[64,1024]{1,0:T(8,128)} custom-call(f32[1024,1024]{1,0:T(8,128)} %emb.1, s32[2,12]{1,0:T(2,128)} %ids_given.1, f32[64,1024]{1,0:T(8,128)} %bitcast.3), custom_call_target="tpu_custom_call" | custom-call | tf_op jit(solution)/shard_map/pallas_call | solution.py:428
  120.8 1.7 %copy.5 = f32[1024,64]{0,1:T(8,128)} copy(f32[1024,64]{0,1:T(8,128)} %bitcast.2) | data formatting | bytes 524288

commit v4 on v3

--- a/solution.py
+++ b/solution.py
@@ -24,7 +24,8 @@
 BF16 = jnp.bfloat16
 F32 = jnp.float32
 
-CHUNKS = ((0, 256), (256, 256), (512, 256), (768, 128), (896, 128))
+CHUNKS = ((0, 256), (256, 256), (512, 256), (768, 256))
+SPLIT = ((0, 768), (768, 256))
 PARTIAL = BF16
 HALF = PTS // 2
 OO, PO, OP, NP, PN = range(5)
@@ -121,8 +122,8 @@
     n_row, n_col,
     emb, ids_given, start, out,
     stage, normed, tiles, x_cols, ids, own_mask, got_mask, masks, deg, deg_sum, near_deg, far_deg,
-    x_half, got_x, factors,
-    scaled, got_scaled, part, got_part, gram, got_gram,
+    x_half, got_x, factors, wide, tall, whole_gram,
+    scaled, got_scaled, part, got_part, gram, half_gram, got_gram,
     load_sem, x_sem, emb_send, emb_recv, mask_send, mask_recv, deg_send, deg_recv, start_send, start_recv,
     vec_send, vec_recv, part_send, part_recv, gram_send, gram_recv,
 ):
@@ -132,10 +133,12 @@
     n_y, n_x = n_row // CORES, n_col // Z_CHIPS
     y, core = row // CORES, lax.rem(row, CORES)
     x, z = col // Z_CHIPS, lax.rem(col, Z_CHIPS)
-    steps = [
-        [(a, b) for a in range(n_y) for b in range(CORES) if a or b],
-        [(a, b) for a in range(n_x) for b in range(Z_CHIPS) if a or b],
-    ]
+    def farthest_first(n_a, n_b):
+        pairs = [(a, b) for a in range(n_a) for b in range(n_b) if a or b]
+        return sorted(pairs, key=lambda s: -min(s[0], n_a - s[0]) - min(s[1], n_b - s[1]))
+
+    steps = [farthest_first(n_y, CORES), farthest_first(n_x, Z_CHIPS), [(0, 1)]]
+    other_core = (y * CORES + (1 - core), col)
     phases = [
         [(lax.rem(y + a, n_y) * CORES + lax.rem(core + b, CORES), col) for a, b in steps[0]],
         [(row, lax.rem(x + a, n_x) * Z_CHIPS + lax.rem(z + b, Z_CHIPS)) for a, b in steps[1]],
@@ -144,7 +147,11 @@
         [steps[0].index((-a % n_y, -b % CORES)) for a, b in steps[0]],
         [steps[1].index((-a % n_x, -b % Z_CHIPS)) for a, b in steps[1]],
     ]
-    base = [0, len(steps[0])]
+    base = [0, len(steps[0]), len(steps[0]) + len(steps[1])]
+    part_rows = K // 2 // CORES
+
+    def rows_of(which):
+        return pl.ds(pl.multiple_of(which * part_rows, part_rows), part_rows)
 
     loads = []
     for i, (begin, count) in enumerate(CHUNKS):
@@ -210,16 +217,18 @@
                 copy.start()
                 mask_copies.append(copy)
         rows = pl.ds(begin, count)
-        for device, side in both:
-            copy = remote(
-                normed.at[OWN, rows],
-                normed.at[PREV + side, rows],
-                emb_send.at[side, i],
-                emb_recv.at[side, i],
-                device,
-            )
-            copy.start()
-            moving[side].append(copy)
+        for first, width in SPLIT if i == len(CHUNKS) - 1 else ((0, D),):
+            for device, side in both:
+                at = len(moving[side])
+                copy = remote(
+                    normed.at[OWN, rows, pl.ds(first, width)],
+                    normed.at[PREV + side, rows, pl.ds(first, width)],
+                    emb_send.at[side, at],
+                    emb_recv.at[side, at],
+                    device,
+                )
+                copy.start()
+                moving[side].append(copy)
         if i == 0:
             x_load.wait()
             x_half[...] = x_cols[...].astype(BF16)
@@ -243,10 +252,14 @@
     left = {OO: OWN, PO: PREV, OP: OWN, NP: NEXT, PN: PREV}
     right = {OO: OWN, PO: OWN, OP: PREV, NP: PREV, PN: NEXT}
 
-    def affinity(tile, r0, r_count, c0, c_count):
-        a = normed[left[tile], pl.ds(r0, r_count), :]
-        b = normed[right[tile], pl.ds(c0, c_count), :]
-        product = lax.dot_general(a, b, (((1,), (1,)), ((), ())), preferred_element_type=F32)
+    def dots(tile, r0, r_count, c0, c_count, first=0, width=D):
+        a = normed[left[tile], pl.ds(r0, r_count), pl.ds(first, width)]
+        b = normed[right[tile], pl.ds(c0, c_count), pl.ds(first, width)]
+        return lax.dot_general(a, b, (((1,), (1,)), ((), ())), preferred_element_type=F32)
+
+    def affinity(tile, r0, r_count, c0, c_count, product=None):
+        if product is None:
+            product = dots(tile, r0, r_count, c0, c_count)
         value = jnp.exp(product * (SHARP / D) - SHARP)
         lists = [masks[pl.ds(2 * tile + block, 1), pl.ds(c0, c_count)] for block in range(BLK_DEV)]
         if r0 < BS < r0 + r_count:
@@ -272,7 +285,7 @@
     spread_mask(NP, theirs, offset_at(2))
     spread_mask(PN, got_mask[1], offset_at(-2))
 
-    for i, (begin, count) in enumerate(CHUNKS):
+    for i, (begin, count) in enumerate(CHUNKS[:-1]):
         moving[0][i].wait_recv()
         affinity(PO, begin, count, 0, PTS)
         affinity(OP, 0, PTS, begin, count)
@@ -283,6 +296,26 @@
         if begin:
             affinity(NP, 0, begin, begin, count)
             affinity(PN, 0, begin, begin, count)
+
+    begin, count = CHUNKS[-1]
+    last = len(CHUNKS) - 1
+    blocks = (
+        (PO, begin, count, 0, PTS, wide.at[0]),
+        (OP, 0, PTS, begin, count, tall.at[0]),
+        (NP, begin, count, 0, PTS, wide.at[1]),
+        (PN, begin, count, 0, PTS, wide.at[2]),
+        (NP, 0, begin, begin, count, tall.at[1, pl.ds(0, begin)]),
+        (PN, 0, begin, begin, count, tall.at[2, pl.ds(0, begin)]),
+    )
+    for part_index, (first, width) in enumerate(SPLIT):
+        moving[0][last + part_index].wait_recv()
+        moving[1][last + part_index].wait_recv()
+        for tile, r0, r_count, c0, c_count, kept in blocks:
+            if part_index == 0:
+                kept[...] = dots(tile, r0, r_count, c0, c_count, first, width)
+            else:
+                total = kept[...] + dots(tile, r0, r_count, c0, c_count, first, width)
+                affinity(tile, r0, r_count, c0, c_count, total)
 
     for place, where in enumerate((PREV, OWN, NEXT)):
         deg_sum[place] = folded(jnp.sum(deg[where], axis=0, keepdims=True))
@@ -309,25 +342,37 @@
         return jnp.dot(vectors, tiles[tile, :, pl.ds(c0, c_count)], preferred_element_type=F32)
 
     def reduce_send(it, phase, packed):
-        gram[it, phase] = packed
         copies = []
-        for k, device in enumerate(phases[phase]):
-            slot = base[phase] + mirror[phase][k]
-            copy = remote(
-                gram.at[it, phase],
-                got_gram.at[it, slot],
-                gram_send.at[it, base[phase] + k],
-                gram_recv.at[it, slot],
-                device,
-            )
+        if phase == 0:
+            gram[it] = packed
+            for k, device in enumerate(phases[0]):
+                theirs = lax.rem(core + steps[0][k][1], CORES)
+                copies.append((gram.at[it, rows_of(theirs)], got_gram, mirror[0][k], k, device))
+        elif phase == 1:
+            half_gram[it] = packed
+            for k, device in enumerate(phases[1]):
+                slot = base[1] + mirror[1][k]
+                copies.append((half_gram.at[it], got_gram, slot, base[1] + k, device))
+        else:
+            whole_gram[it, rows_of(core), :] = packed
+            mine = whole_gram.at[it, rows_of(core)]
+            copies.append((mine, None, base[2], base[2], other_core))
+        started = []
+        for src, landing, slot, k, device in copies:
+            dst = src if landing is None else landing.at[it, slot]
+            copy = remote(src, dst, gram_send.at[it, k], gram_recv.at[it, slot], device)
             copy.start()
-            copies.append(copy)
-        sent_only.extend(copies)
-        return copies
+            started.append(copy)
+        sent_only.extend(started)
+        return started
 
     def reduce_wait(it, phase, packed, copies):
         for copy in copies:
             copy.wait_recv()
+        if phase == 2:
+            return whole_gram[it]
+        if phase == 0:
+            packed = gram[it, rows_of(core), :]
         for k in range(len(phases[phase])):
             packed = packed + got_gram[it, base[phase] + k]
         return packed
@@ -386,6 +431,7 @@
         sent_only.extend(part_copies)
         total = total + product(from_prev, PO, 0, PTS)
         beside(2)
+        beside(3)
         for copy in part_copies:
             copy.wait_recv()
         halves = [
@@ -403,7 +449,7 @@
                 state["sum"] = gram_packed(image)
             else:
                 state["sum"] = reduce_wait(it - 1, stage_index - 1, state["sum"], state["copies"])
-            if stage_index < len(phases):
+            if stage_index < 3:
                 state["copies"] = reduce_send(it - 1, stage_index, state["sum"])
             else:
                 factors[it - 1] = inverse_factor(state["sum"]) * scale
@@ -412,7 +458,7 @@
         image = apply_factor(factors[it - 1], following)
 
     packed = gram_packed(image)
-    for phase in range(len(phases)):
+    for phase in range(3):
         copies = reduce_send(ITERS - 1, phase, packed)
         packed = reduce_wait(ITERS - 1, phase, packed, copies)
     result = apply_factor(inverse_factor(packed) * scale, image)
@@ -423,8 +469,8 @@
 
 
 def on_device(n_row, n_col, embeddings, neighbour_ids, start_vectors):
-    sums = n_row - 1 + n_col - 1
-    n_chunks = len(CHUNKS)
+    sums = n_row - 1 + n_col - 1 + 1
+    n_chunks = len(CHUNKS) + len(SPLIT) - 1
     return pl.pallas_call(
         functools.partial(kernel, n_row, n_col),
         out_shape=jax.ShapeDtypeStruct((K, PTS), F32),
@@ -450,12 +496,16 @@
             pltpu.VMEM((K, PTS), BF16),
             pltpu.VMEM((2, K, PTS), BF16),
             pltpu.VMEM((ITERS - 1, K, K), F32),
+            pltpu.VMEM((3, CHUNKS[-1][1], PTS), F32),
+            pltpu.VMEM((3, PTS, CHUNKS[-1][1]), F32),
+            pltpu.VMEM((ITERS, K // 2, 2 * K), F32),
             pltpu.VMEM((ITERS - 1, K, PTS), BF16),
             pltpu.VMEM((ITERS - 1, 2, K, PTS), BF16),
             pltpu.VMEM((ITERS, 2, 2, K, HALF), PARTIAL),
             pltpu.VMEM((ITERS, 2, 2, K, HALF), PARTIAL),
-            pltpu.VMEM((ITERS, 2, K // 2, 2 * K), F32),
-            pltpu.VMEM((ITERS, sums, K // 2, 2 * K), F32),
+            pltpu.VMEM((ITERS, K // 2, 2 * K), F32),
+            pltpu.VMEM((ITERS, K // 2 // CORES, 2 * K), F32),
+            pltpu.VMEM((ITERS, sums, K // 2 // CORES, 2 * K), F32),
             pltpu.SemaphoreType.DMA((n_chunks,)),
             pltpu.SemaphoreType.DMA((2,)),
             pltpu.SemaphoreType.DMA((2, n_chunks)),

time: 123 us -> 118 us (0.959)
  Pallas kernels: 121 us -> 116 us
    pallas_call x1, Pallas kernels: 121 us -> 116 us  [on_device(): pl.pallas_call(functools.partial(kernel, n_row, n_col), out_shape=jax.Sha...]
where the time goes in v4:
time: 118 us; the launch traced here: 117 us
  Pallas kernels  116 us (98%)
  local copies, waits for them, and re-layouts  1.67 us (1%)
    pallas_call x1, Pallas kernels, on_device(): pl.pallas_call(functools.partial(kernel, n_row, n_col), out_shape=jax.Sha...  116 us

profile of v4, /device:TPU:1, one launch (start us, length us, event | category | flops | bytes accessed | tf_op | source)
XLA Modules:
  0.0 117.4 jit_solution(5320451737007778353)
XLA Ops:
  0.0 115.7 %shard_map.37 = f32[64,1024]{1,0:T(8,128)} custom-call(f32[1024,1024]{1,0:T(8,128)} %emb.1, s32[2,12]{1,0:T(2,128)} %ids_given.1, f32[64,1024]{1,0:T(8,128)} %bitcast.3), custom_call_target="tpu_custom_call" | custom-call | tf_op jit(solution)/shard_map/pallas_call | solution.py:474
  115.7 1.7 %copy.5 = f32[1024,64]{0,1:T(8,128)} copy(f32[1024,64]{0,1:T(8,128)} %bitcast.2) | data formatting | bytes 524288

commit v5 on v4

--- a/solution.py
+++ b/solution.py
@@ -229,13 +229,12 @@
                 )
                 copy.start()
                 moving[side].append(copy)
-        if i == 0:
-            x_load.wait()
-            x_half[...] = x_cols[...].astype(BF16)
-            for device, side in both:
-                copy = remote(x_half, got_x.at[side], start_send.at[side], start_recv.at[side], device)
-                copy.start()
-                start_copies.append(copy)
+    x_load.wait()
+    x_half[...] = x_cols[...].astype(BF16)
+    for device, side in both:
+        copy = remote(x_half, got_x.at[side], start_send.at[side], start_recv.at[side], device)
+        copy.start()
+        start_copies.append(copy)
 
     first_block = lax.broadcasted_iota(jnp.int32, (1, PTS), 1) < BS
 
@@ -384,7 +383,6 @@
         return (got_x[side].astype(F32) * inverse).astype(BF16)
 
     def apply_affinity(it, vectors, beside):
-        beside(0)
         own_scaled = (vectors * inv_root).astype(BF16)
         copies = []
         if it:
@@ -400,7 +398,9 @@
                 copy.start()
                 copies.append(copy)
             sent_only.extend(copies)
-        total = product(own_scaled, OO, 0, PTS)
+        beside(0)
+        if it:
+            total = product(own_scaled, OO, 0, PTS)
         to_prev = product(own_scaled, OP, 0, PTS)
         beside(1)
         if it:
@@ -429,6 +429,8 @@
                 copy.start()
                 part_copies.append(copy)
         sent_only.extend(part_copies)
+        if not it:
+            total = product(own_scaled, OO, 0, PTS)
         total = total + product(from_prev, PO, 0, PTS)
         beside(2)
         beside(3)

time: 118 us -> 115 us (0.975)
  Pallas kernels: 116 us -> 113 us
    pallas_call x1, Pallas kernels: 116 us -> 113 us  [on_device(): pl.pallas_call(functools.partial(kernel, n_row, n_col), out_shape=jax.Sha...]
where the time goes in v5:
time: 115 us
  Pallas kernels  113 us (98%)
  local copies, waits for them, and re-layouts  1.67 us (1%)
    pallas_call x1, Pallas kernels, on_device(): pl.pallas_call(functools.partial(kernel, n_row, n_col), out_shape=jax.Sha...  113 us

profile of v5, /device:TPU:1, one launch (start us, length us, event | category | flops | bytes accessed | tf_op | source)
XLA Modules:
  0.0 114.8 jit_solution(4533765376684970045)
XLA Ops:
  0.0 113.1 %shard_map.37 = f32[64,1024]{1,0:T(8,128)} custom-call(f32[1024,1024]{1,0:T(8,128)} %emb.1, s32[2,12]{1,0:T(2,128)} %ids_given.1, f32[64,1024]{1,0:T(8,128)} %bitcast.3), custom_call_target="tpu_custom_call" | custom-call | tf_op jit(solution)/shard_map/pallas_call | solution.py:476
  113.2 1.7 %copy.5 = f32[1024,64]{0,1:T(8,128)} copy(f32[1024,64]{0,1:T(8,128)} %bitcast.2) | data formatting | bytes 524288

commit v6 on v5

--- a/solution.py
+++ b/solution.py
@@ -25,7 +25,7 @@
 F32 = jnp.float32
 
 CHUNKS = ((0, 256), (256, 256), (512, 256), (768, 256))
-SPLIT = ((0, 768), (768, 256))
+SPLIT = ((0, 512), (512, 256), (768, 256))
 PARTIAL = BF16
 HALF = PTS // 2
 OO, PO, OP, NP, PN = range(5)
@@ -299,35 +299,51 @@
     begin, count = CHUNKS[-1]
     last = len(CHUNKS) - 1
     blocks = (
+        (PN, begin, count, 0, PTS, wide.at[2]),
+        (PN, 0, begin, begin, count, tall.at[2, pl.ds(0, begin)]),
+        (NP, begin, count, 0, PTS, wide.at[1]),
+        (NP, 0, begin, begin, count, tall.at[1, pl.ds(0, begin)]),
+        (OP, 0, PTS, begin, count, tall.at[0]),
         (PO, begin, count, 0, PTS, wide.at[0]),
-        (OP, 0, PTS, begin, count, tall.at[0]),
-        (NP, begin, count, 0, PTS, wide.at[1]),
-        (PN, begin, count, 0, PTS, wide.at[2]),
-        (NP, 0, begin, begin, count, tall.at[1, pl.ds(0, begin)]),
-        (PN, 0, begin, begin, count, tall.at[2, pl.ds(0, begin)]),
     )
-    for part_index, (first, width) in enumerate(SPLIT):
+    for part_index, (first, width) in enumerate(SPLIT[:-1]):
         moving[0][last + part_index].wait_recv()
         moving[1][last + part_index].wait_recv()
         for tile, r0, r_count, c0, c_count, kept in blocks:
-            if part_index == 0:
-                kept[...] = dots(tile, r0, r_count, c0, c_count, first, width)
-            else:
-                total = kept[...] + dots(tile, r0, r_count, c0, c_count, first, width)
-                affinity(tile, r0, r_count, c0, c_count, total)
-
-    for place, where in enumerate((PREV, OWN, NEXT)):
-        deg_sum[place] = folded(jnp.sum(deg[where], axis=0, keepdims=True))
+            partly = dots(tile, r0, r_count, c0, c_count, first, width)
+            kept[...] = kept[...] + partly if part_index else partly
+
     far_prev = (row, lax.rem(col + n_col - 2, n_col))
     far_next = (row, lax.rem(col + 2, n_col))
-    deg_copies = [
-        remote(deg_sum.at[pl.ds(1, 2)], near_deg.at[0], deg_send.at[0], deg_recv.at[0], nxt),
-        remote(deg_sum.at[pl.ds(0, 2)], near_deg.at[1], deg_send.at[1], deg_recv.at[1], prev),
-        remote(deg_sum.at[2], far_deg.at[0], deg_send.at[2], deg_recv.at[2], far_next),
-        remote(deg_sum.at[0], far_deg.at[1], deg_send.at[3], deg_recv.at[3], far_prev),
-    ]
-    for copy in deg_copies:
-        copy.start()
+    deg_copies = []
+
+    def send_degrees(place, where, copies):
+        deg_sum[place] = folded(jnp.sum(deg[where], axis=0, keepdims=True))
+        for copy in copies:
+            copy.start()
+        deg_copies.extend(copies)
+
+    moving[0][-1].wait_recv()
+    moving[1][-1].wait_recv()
+    for tile, r0, r_count, c0, c_count, kept in blocks:
+        total = kept[...] + dots(tile, r0, r_count, c0, c_count, *SPLIT[-1])
+        affinity(tile, r0, r_count, c0, c_count, total)
+        if tile == PN and r0 == 0:
+            send_degrees(
+                2, NEXT, [remote(deg_sum.at[2], far_deg.at[0], deg_send.at[2], deg_recv.at[2], far_next)]
+            )
+        if tile == OP:
+            send_degrees(
+                0, PREV, [remote(deg_sum.at[0], far_deg.at[1], deg_send.at[3], deg_recv.at[3], far_prev)]
+            )
+    send_degrees(
+        1,
+        OWN,
+        [
+            remote(deg_sum.at[pl.ds(1, 2)], near_deg.at[0], deg_send.at[0], deg_recv.at[0], nxt),
+            remote(deg_sum.at[pl.ds(0, 2)], near_deg.at[1], deg_send.at[1], deg_recv.at[1], prev),
+        ],
+    )
     for copy in start_copies + deg_copies:
         copy.wait_recv()
     inv_root = unfolded(lax.rsqrt(deg_sum[1] + near_deg[0, 1] + near_deg[1, 0]))

time: 115 us -> 115 us (level)
  no operation moved by 1% of the time
where the time goes in v6:
time: 115 us
  Pallas kernels  113 us (98%)
  local copies, waits for them, and re-layouts  1.67 us (1%)
    pallas_call x1, Pallas kernels, on_device(): pl.pallas_call(functools.partial(kernel, n_row, n_col), out_shape=jax.Sha...  113 us

profile of v6, /device:TPU:1, one launch (start us, length us, event | category | flops | bytes accessed | tf_op | source)
XLA Modules:
  0.0 114.8 jit_solution(16438092916987932953)
XLA Ops:
  0.0 113.2 %shard_map.37 = f32[64,1024]{1,0:T(8,128)} custom-call(f32[1024,1024]{1,0:T(8,128)} %emb.1, s32[2,12]{1,0:T(2,128)} %ids_given.1, f32[64,1024]{1,0:T(8,128)} %bitcast.3), custom_call_target="tpu_custom_call" | custom-call | tf_op jit(solution)/shard_map/pallas_call | solution.py:492
  113.2 1.7 %copy.5 = f32[1024,64]{0,1:T(8,128)} copy(f32[1024,64]{0,1:T(8,128)} %bitcast.2) | data formatting | bytes 524288

commit v7 on v6

--- a/solution.py
+++ b/solution.py
@@ -417,7 +417,7 @@
         beside(0)
         if it:
             total = product(own_scaled, OO, 0, PTS)
-        to_prev = product(own_scaled, OP, 0, PTS)
+            to_prev = product(own_scaled, OP, 0, PTS)
         beside(1)
         if it:
             for copy in copies:
@@ -432,7 +432,10 @@
                 if side == 0:
                     piece = product(from_prev, PN, half * HALF, HALF)
                 else:
-                    piece = to_prev[:, half * HALF : (half + 1) * HALF]
+                    if it:
+                        piece = to_prev[:, half * HALF : (half + 1) * HALF]
+                    else:
+                        piece = product(own_scaled, OP, half * HALF, HALF)
                     piece = piece + product(from_next, NP, half * HALF, HALF)
                 part[it, side, half] = piece.astype(PARTIAL)
                 copy = remote(

time: 115 us -> 115 us (level)
  no operation moved by 1% of the time
where the time goes in v7:
time: 115 us
  Pallas kernels  113 us (98%)
  local copies, waits for them, and re-layouts  1.67 us (1%)
    pallas_call x1, Pallas kernels, on_device(): pl.pallas_call(functools.partial(kernel, n_row, n_col), out_shape=jax.Sha...  113 us

profile of v7, /device:TPU:1, one launch (start us, length us, event | category | flops | bytes accessed | tf_op | source)
XLA Modules:
  0.0 115.0 jit_solution(10664447048989887782)
XLA Ops:
  0.0 113.3 %shard_map.37 = f32[64,1024]{1,0:T(8,128)} custom-call(f32[1024,1024]{1,0:T(8,128)} %emb.1, s32[2,12]{1,0:T(2,128)} %ids_given.1, f32[64,1024]{1,0:T(8,128)} %bitcast.3), custom_call_target="tpu_custom_call" | custom-call | tf_op jit(solution)/shard_map/pallas_call | solution.py:495
  113.3 1.7 %copy.5 = f32[1024,64]{0,1:T(8,128)} copy(f32[1024,64]{0,1:T(8,128)} %bitcast.2) | data formatting | bytes 524288
